TPU v7x, 32 devices: a whole 2x2x4 slice. The times are simulated.
32 devices in a mesh: dp: 4 (over x, core), chan: 8 (over z, y).
Axes of the slice: x: 2, y: 2, z: 4, core: 2. Of those that a mesh axis runs over, the one named last changes fastest.
Arguments:
- features: bfloat16 [512, 2, 128, 256], P('chan', None, 'dp'), may hold values from -6 to 6
- latent: bfloat16 [2, 512], replicated, may hold values from -6 to 6
- affine: bfloat16 [512, 512], replicated, may hold values from -0.25 to 0.25
- affine_bias: float32 [512], replicated, may hold values from 0.5 to 1.5
- weight: bfloat16 [3, 3, 512, 512], P(None, None, 'chan'), may hold values from -0.09375 to 0.09375
- out_bias: float32 [512], P('chan'), may hold values from -3 to 3
- cotangent: bfloat16 [512, 2, 128, 256], P('chan', None, 'dp'), may hold values from -6 to 6
- latents_all: bfloat16 [2048, 512], P(('dp', 'chan')), may hold values from -6 to 6
- labels: int32 [2048], P(('dp', 'chan')), may hold values from 0 to 999
- class_means: float32 [1000, 512], replicated, may hold values from -6 to 6
Outputs:
- output: bfloat16 [512, 2, 128, 256], P('chan', None, 'dp')
- grad_features: float32 [512, 2, 128, 256], P('chan', None, 'dp')
- grad_latent: float32 [2, 512], replicated
- grad_affine: float32 [512, 512], replicated
- grad_affine_bias: float32 [512], replicated
- grad_weight: float32 [3, 3, 512, 512], P(None, None, 'chan')
- grad_bias: float32 [512], P('chan')
- class_target: float32 [1000, 512], replicated
All inputs are finite; a program needn't handle non-finite values.
Results may differ from a plain program's by a relative error of at most 0.0053.
Values may be sent and summed in bfloat16 or wider, within the bound.
No kernel may reach another device: no remote copies, remote signals or barrier semaphores. Data moves between devices by JAX's collectives and lax.ppermute only.
A program may use at most 512 MiB of HBM per device.

v0:
```python
import functools

import jax
import jax.numpy as jnp
import ml_dtypes
import numpy as np
from jax import lax
from jax.experimental import pallas as pl
from jax.experimental.pallas import tpu as pltpu
from jax.sharding import PartitionSpec as P

F32 = jnp.float32
BF16 = jnp.bfloat16
IN_VMEM = pl.BlockSpec(memory_space=pltpu.VMEM)
IN_HBM = pl.BlockSpec(memory_space=pltpu.HBM)
IN_SMEM = pl.BlockSpec(memory_space=pltpu.SMEM)
PARAMS = pltpu.CompilerParams(vmem_limit_bytes=60 << 20)
RIM = 7
GROUP = 16


def struct(shape, dtype):
    return jax.ShapeDtypeStruct(shape, dtype)


def sinc_taps():
    offset = np.arange(12) - 5.5
    values = np.sinc(offset * 0.5) * (0.5 + 0.5 * np.cos(np.pi * offset / 6.0))
    return values / values.sum()


def up_table(size):
    tap = np.arange(2 * size)[None, :] - 2 * np.arange(size)[:, None] + 5
    held = (tap >= 0) & (tap < 12)
    return np.where(held, 2.0 * sinc_taps()[np.clip(tap, 0, 11)], 0.0).astype(np.float32)


def halves(table):
    high = table.astype(ml_dtypes.bfloat16)
    return [high, (table - high.astype(np.float32)).astype(ml_dtypes.bfloat16)]


def from_neighbours(value, axis, dim, width):
    size, length = lax.axis_size(axis), value.shape[dim]
    up = [(i, i + 1) for i in range(size - 1)]
    down = [(j, i) for i, j in up]
    last = lax.slice_in_dim(value, length - width, length, axis=dim)
    first = lax.slice_in_dim(value, 0, width, axis=dim)
    return lax.ppermute(last, axis, up), lax.ppermute(first, axis, down)


def swapped(value, axis, bits):
    return lax.ppermute(value, axis, [(i, i ^ bits) for i in range(lax.axis_size(axis))])


def once(value, *others):
    return lax.optimization_barrier((value,) + others)[0]


def order(count, kind):
    far, near = list(range(4, count)), list(range(1, min(4, count)))
    if kind == "far":
        return [0] + far + near
    if kind == "near":
        return [0] + near + far
    mixed = [x for pair in zip(far, near) for x in pair]
    return [0] + mixed + far[len(near) :] + near[len(far) :]


def exchange(parts, kind):
    steps = order(lax.axis_size("chan"), kind)
    return [parts[0]] + [swapped(part, "chan", x) for part, x in zip(parts[1:], steps[1:])]


def started(sems, first, pairs):
    copies = [
        pltpu.make_async_copy(source, target, sems.at[first + index])
        for index, (source, target) in enumerate(pairs)
    ]
    for copy in copies:
        copy.start()
    return copies


def finished(copies):
    for copy in copies:
        copy.wait()


def rows_kernel(count, me_ref, before, value, after, *refs):
    parts, (arrived, rows_first, sems) = refs[:count], refs[count:]
    me = me_ref[0]
    width, items, rows, _ = value.shape
    blocks = count // items
    span = rows // blocks
    finished(started(sems, 0, [(value, arrived)]))
    for item in range(items):
        for group in range(width // GROUP):
            at = slice(group * GROUP, (group + 1) * GROUP)
            rows_first[item, 1 : rows + 1, at] = jnp.swapaxes(arrived[at, item], 0, 1)
        rows_first[item, 0] = before[:, item, 0]
        rows_first[item, rows + 1] = after[:, item, 0]
    pairs = []
    for x, part in zip(order(count, "far"), parts):
        dest = me ^ x
        start = (dest % blocks) * span
        pairs.append((rows_first.at[dest // blocks, pl.ds(start, span + 2)], part))
    finished(started(sems, 1, pairs))


def row_parts(me, before, value, after, count):
    width, items, rows, columns = value.shape
    span = rows * items // count
    return pl.pallas_call(
        functools.partial(rows_kernel, count),
        out_shape=[struct((span + 2, width, columns), BF16)] * count,
        in_specs=[IN_SMEM, IN_VMEM, IN_HBM, IN_VMEM],
        out_specs=[IN_HBM] * count,
        scratch_shapes=[
            pltpu.VMEM((width, items, rows, columns), BF16),
            pltpu.VMEM((items, rows + 2, width, columns), BF16),
            pltpu.SemaphoreType.DMA((1 + count,)),
        ],
        compiler_params=PARAMS,
        name="row_parts",
    )(me, before, value, after)


def weight_pieces(weight, me_dp):
    shares = min(lax.axis_size("dp"), weight.shape[3] // 128)
    share = weight.shape[3] // shares
    held = lax.dynamic_slice_in_dim(weight, me_dp % shares * share, share, 3).reshape(1, 9, -1, share)
    places = [(0, 0)]
    bit = lax.axis_size("chan") // 2
    while bit >= 4:
        held = jnp.concatenate([held, swapped(held, "chan", bit)], axis=0)
        places += [(chan ^ bit, dp) for chan, dp in places]
        bit //= 2
    return held, places


def near_pieces(held, places):
    near = range(1, min(lax.axis_size("chan"), 4))
    held = jnp.concatenate([held] + [swapped(held, "chan", x) for x in near], axis=0)
    return held, places + [(chan ^ x, dp) for x in near for chan, dp in places]


def met_pieces(held, places, bit):
    return swapped(held, "dp", bit), [(chan, dp ^ bit) for chan, dp in places]


def tap_blocks(me, part, pieces, places, taps):
    share = pieces[0].shape[3]
    pairs = []
    for piece, blocks in zip(pieces, places):
        for index, (chan, dp) in enumerate(blocks):
            lanes = pl.ds(pl.multiple_of((part ^ dp) * share, share), share)
            pairs.append((piece.at[index], taps.at[:, me ^ chan, :, lanes]))
    return pairs


def transposed_kernel(places, me_ref, part_ref, *refs):
    pieces, (out, taps, turned, sems) = refs[:-4], refs[-4:]
    pairs = tap_blocks(me_ref[0], part_ref[0], pieces, places, taps)
    finished(started(sems, 0, pairs))
    channels = taps.shape[3]
    copies = []
    for tap in range(9):
        turned[8 - tap] = jnp.transpose(taps[tap].reshape(channels, channels))
        copies += started(sems, len(pairs) + tap, [(turned.at[8 - tap], out.at[8 - tap])])
    finished(copies)


def transposed_taps(me, part, pieces, places, channels):
    own = pieces[0].shape[2]
    blocks = sum(len(place) for place in places)
    return pl.pallas_call(
        functools.partial(transposed_kernel, places),
        out_shape=struct((9, channels, channels), BF16),
        in_specs=[IN_SMEM, IN_SMEM] + [IN_HBM] * len(pieces),
        out_specs=IN_HBM,
        scratch_shapes=[
            pltpu.VMEM((9, channels // own, own, channels), BF16),
            pltpu.VMEM((9, channels, channels), BF16),
            pltpu.SemaphoreType.DMA((blocks + 9,)),
        ],
        compiler_params=PARAMS,
        name="transposed_taps",
    )(me, part, *pieces)


def arrivals(me, parts, arrived):
    count, _, own, _ = arrived.shape
    width = parts[0].shape[1]
    steps = order(count, "near" if width < own else "far")
    return [
        (part, arrived.at[me ^ steps[index % count], :, pl.ds(index // count * width, width)])
        for index, part in enumerate(parts)
    ]


def departures(me, results, outs, kind):
    count = results.shape[1]
    return [(results.at[:, me ^ x], out) for x, out in zip(order(count, kind), outs)]


def fill_shifted(arrived, scales, shifted):
    count, rows, own, columns = arrived.shape

    def row_step(row, carry):
        column = lax.broadcasted_iota(jnp.int32, (own, columns), 1)
        for source in range(count):
            value = arrived[source, row].astype(F32)
            if scales is not None:
                value = (value * scales[source]).astype(BF16).astype(F32)
            before = jnp.where(column == 0, 0.0, pltpu.roll(value, 1, 1))
            after = jnp.where(column == columns - 1, 0.0, pltpu.roll(value, columns - 1, 1))
            shifted[row, 0, source] = before.astype(BF16)
            shifted[row, 1, source] = value.astype(BF16)
            shifted[row, 2, source] = after.astype(BF16)
        return carry

    lax.fori_loop(0, rows, row_step, 0)


def convolved(taps, shifted, row, channels, columns):
    total = None
    for i in range(3):
        for j in range(3):
            term = jnp.dot(
                taps[3 * i + j].reshape(channels, channels),
                shifted[row + i, j].reshape(channels, columns),
                preferred_element_type=F32,
            )
            total = term if total is None else total + term
    return total


def forward_kernel(count, places, me_ref, part_ref, scales, *refs):
    pieces, refs = refs[: len(places)], refs[len(places) :]
    parts, outs = refs[:count], refs[count:-7]
    arrived, shifted, taps, results, wide_scales, sems, row_sems = refs[-7:]
    me = me_ref[0]
    rows, _, own, columns = results.shape
    arriving = started(sems, 0, arrivals(me, parts, arrived))
    tapping = started(sems, count, tap_blocks(me, part_ref[0], pieces, places, taps))
    wide_scales[...] = jnp.broadcast_to(scales[...], wide_scales.shape)
    finished(arriving)
    fill_shifted(arrived, wide_scales, shifted)
    finished(tapping)

    def leaving(row):
        return [
            pltpu.make_async_copy(results.at[row, me ^ x], out.at[row], row_sems.at[row, x])
            for x, out in zip(order(count, "mixed"), outs)
        ]

    def row_step(row, carry):
        total = convolved(taps, shifted, row, count * own, columns)
        results[row] = total.astype(BF16).reshape(count, own, columns)
        for copy in leaving(row):
            copy.start()
        return carry

    lax.fori_loop(0, rows, row_step, 0, unroll=min(4, rows))
    for row in range(rows):
        finished(leaving(row))


def conv_forward(me, part, pieces, places, scales, parts):
    count = len(parts)
    rows, own, columns = parts[0].shape
    blocks = sum(len(place) for place in places)
    return pl.pallas_call(
        functools.partial(forward_kernel, count, places),
        out_shape=[struct((rows - 2, own, columns), BF16)] * count,
        in_specs=[IN_SMEM, IN_SMEM, IN_VMEM] + [IN_HBM] * (len(pieces) + count),
        out_specs=[IN_HBM] * count,
        scratch_shapes=[
            pltpu.VMEM((count, rows, own, columns), BF16),
            pltpu.VMEM((rows, 3, count, own, columns), BF16),
            pltpu.VMEM((9, count, own, count * own), BF16),
            pltpu.VMEM((rows - 2, count, own, columns), BF16),
            pltpu.VMEM((count, own, columns), F32),
            pltpu.SemaphoreType.DMA((count + blocks,)),
            pltpu.SemaphoreType.DMA((rows - 2, count)),
        ],
        compiler_params=PARAMS,
        name="conv_forward",
    )(me, part, scales, *pieces, *parts)


def backward_kernel(count, split, me_ref, scales, taps_ref, _, *refs):
    grads, refs = refs[: count * split], refs[count * split :]
    feats, outs, (style_ref, weight_out) = refs[:count], refs[count : 2 * count], refs[2 * count : 2 * count + 2]
    arrived, arrived_feats, shifted, modded, taps, results, weight_sums, wide_scales, sems = refs[2 * count + 2 :]
    me = me_ref[0]
    rows, _, own, columns = results.shape
    channels = count * own
    shares, _, _, share = weight_sums.shape
    arriving = started(sems, 0, arrivals(me, grads, arrived))
    tapping = started(
        sems,
        count * split,
        [(taps_ref, taps)] + arrivals(me, feats, arrived_feats),
    )
    wide_scales[...] = jnp.broadcast_to(scales[...], wide_scales.shape)
    finished(arriving)
    fill_shifted(arrived, None, shifted)
    finished(tapping)
    style_ref[...] = jnp.zeros_like(style_ref)

    def row_step(row, carry):
        total = convolved(taps, shifted, row, channels, columns).reshape(count, own, columns)
        results[row] = total.astype(BF16)
        product = total * arrived_feats[:, row + 1].astype(F32)
        style_ref[...] += jnp.sum(product, axis=2, keepdims=True)
        return carry

    lax.fori_loop(0, rows, row_step, 0, unroll=min(4, rows))
    leaving = started(sems, 0, departures(me, results, outs, "far"))

    def modded_step(row, carry):
        for source in range(count):
            value = arrived_feats[source, row].astype(F32) * wide_scales[source]
            modded[row, source] = value.astype(BF16)
        return carry

    lax.fori_loop(0, rows + 2, modded_step, 0)

    def weight_leaving(tap):
        return pltpu.make_async_copy(weight_sums.at[:, tap], weight_out.at[:, tap], sems.at[count + tap])

    def tap_step(tap, carry):
        i, j = lax.div(tap, 3), lax.rem(tap, 3)
        total = None
        for row in range(rows):
            term = lax.dot_general(
                shifted[row + 1, 2 - j].reshape(channels, columns),
                modded[row + i].reshape(channels, columns),
                (((1,), (1,)), ((), ())),
                preferred_element_type=F32,
            )
            total = term if total is None else total + term
        total = total.astype(BF16)
        for index in range(shares):
            weight_sums[index, tap] = total[:, index * share : (index + 1) * share]
        weight_leaving(tap).start()
        return carry

    lax.fori_loop(0, 9, tap_step, 0, unroll=3)
    finished(leaving + [weight_leaving(tap) for tap in range(9)])


def conv_backward(me, scales, taps, earlier, grads, feats, shares):
    count = len(feats)
    split = len(grads) // count
    rows, own, columns = feats[0].shape
    channels = count * own
    share = channels // shares
    outs = pl.pallas_call(
        functools.partial(backward_kernel, count, split),
        out_shape=[struct((rows - 2, own, columns), BF16)] * count
        + [struct((count, own, 1), F32), struct((shares, 9, channels, share), BF16)],
        in_specs=[IN_SMEM, IN_VMEM] + [IN_HBM] * (2 + len(grads) + count),
        out_specs=[IN_HBM] * count + [IN_VMEM, IN_HBM],
        scratch_shapes=[
            pltpu.VMEM((count, rows, own, columns), BF16),
            pltpu.VMEM((count, rows, own, columns), BF16),
            pltpu.VMEM((rows, 3, count, own, columns), BF16),
            pltpu.VMEM((rows, count, own, columns), BF16),
            pltpu.VMEM((9, channels, channels), BF16),
            pltpu.VMEM((rows - 2, count, own, columns), BF16),
            pltpu.VMEM((shares, 9, channels, share), BF16),
            pltpu.VMEM((count, own, columns), F32),
            pltpu.SemaphoreType.DMA((count + max(9, len(grads) + 1),)),
        ],
        compiler_params=PARAMS,
        name="conv_backward",
    )(me, scales, taps, earlier, *grads, *feats)
    return outs[:-2], outs[-2], outs[-1]


def finish_kernel(shares, part_ref, weight, factors, *refs):
    pieces, (out, arrived, sems) = refs[:shares], refs[shares:]
    part = part_ref[0]
    share = pieces[0].shape[1]
    taps, own, _ = out.shape
    pairs = []
    for x, piece in enumerate(pieces):
        lanes = pl.ds(pl.multiple_of((part ^ x) * share, share), share)
        pairs.append((piece.at[pl.ds(0, taps * own)], arrived.at[:, lanes]))
    finished(started(sems, 0, pairs))
    twice = 2.0 * factors[...]
    for tap in range(taps):
        out[tap] = arrived[tap * own : (tap + 1) * own].astype(F32) + twice * weight[tap].astype(F32)


def finished_weight(part, weight, factors, pieces):
    _, own, channels = weight.shape
    shares = len(pieces)
    return pl.pallas_call(
        functools.partial(finish_kernel, shares),
        out_shape=struct((9, own, channels), F32),
        in_specs=[IN_SMEM, IN_VMEM, IN_VMEM] + [IN_HBM] * shares,
        out_specs=IN_VMEM,
        scratch_shapes=[
            pltpu.VMEM((9 * own, channels), BF16),
            pltpu.SemaphoreType.DMA((shares,)),
        ],
        compiler_params=PARAMS,
        name="finished_weight",
    )(part, weight, factors, *pieces)


def row_blocks(me, parts, rows_ref, start, kind, first_channel=0):
    count = len(parts)
    blocks = count // rows_ref.shape[0]
    span = parts[0].shape[0]
    pairs = []
    channels = pl.ds(first_channel, rows_ref.shape[2])
    for x, part in zip(order(count, kind), parts):
        source = me ^ x
        at = pl.ds(start + (source % blocks) * span, span)
        pairs.append((part.at[:, channels], rows_ref.at[source // blocks, at]))
    return pairs


def rims_kernel(count, me_ref, *refs):
    parts, (first, last, arrived, sems) = refs[:count], refs[-4:]
    rows = arrived.shape[1]
    finished(started(sems, 0, row_blocks(me_ref[0], parts, arrived, 0, "mixed")))
    pairs = [
        (arrived.at[:, pl.ds(0, RIM)], first),
        (arrived.at[:, pl.ds(rows - RIM, RIM)], last),
    ]
    finished(started(sems, count, pairs))


def rims(me, parts, items, earlier):
    count = len(parts)
    span, width, columns = parts[0].shape
    rim = struct((items, RIM, width, columns), BF16)
    return pl.pallas_call(
        functools.partial(rims_kernel, count),
        out_shape=[rim, rim],
        in_specs=[IN_SMEM] + [IN_HBM] * (count + len(earlier)),
        out_specs=[IN_HBM] * 2,
        scratch_shapes=[
            pltpu.VMEM((items, span * count // items, width, columns), BF16),
            pltpu.SemaphoreType.DMA((count + 2,)),
        ],
        compiler_params=PARAMS,
        name="rims",
    )(me, *parts, *earlier)


def sinc_tile(rows, edges, wide, wide_grad, narrow):
    backward = wide_grad is not None
    spare = 1 if backward else 0
    tap = [float(value) for value in sinc_taps()[:6]]
    sums, picked = [{}, {}], {}
    for row in range(rows + 2 * RIM):
        for which, load in enumerate((wide, wide_grad) if backward else (wide,)):
            value = load(row)
            products = [value * (2.0 * tap[t]) for t in range(6)]
            for offset in range(-3, 4):
                pair = row - RIM + offset
                for parity in range(2):
                    t = 2 * offset + parity + 5
                    if -3 - spare <= pair < rows + 3 + spare and 0 <= t < 12:
                        term = products[min(t, 11 - t)]
                        key = 2 * pair + parity
                        sums[which][key] = sums[which][key] + term if key in sums[which] else term
        pair = row - RIM - 3
        if not -3 - spare <= pair < rows + 3 + spare:
            continue
        for key in (2 * pair, 2 * pair + 1):
            value = sums[0].pop(key)
            sigmoid = 0.5 + 0.5 * jnp.tanh(0.5 * value)
            result = value * sigmoid
            if backward:
                result = sums[1].pop(key) * (sigmoid + result * (1.0 - sigmoid))
            if pair < 0:
                result = result * edges[0]
            if pair >= rows:
                result = result * edges[1]
            picked[key] = result
        centre = pair - 3
        if -spare <= centre < rows + spare:
            total = None
            for t in range(6):
                term = tap[t] * (picked[2 * centre + t - 5] + picked[2 * centre + 6 - t])
                total = term if total is None else total + term
            narrow(centre + spare, total)
        for key in (2 * centre - 6, 2 * centre - 5, 2 * centre - 4):
            picked.pop(key, None)


def widened(values, up):
    columns = values.shape[-1]
    flat = values.reshape(-1, columns)
    total = jnp.dot(jnp.concatenate([flat, flat], axis=1), up, preferred_element_type=F32)
    return total.reshape(-1, GROUP, 2 * columns)


def narrowed(values, down):
    columns = values.shape[-1]
    flat = values.reshape(-1, columns)
    high = flat.astype(BF16)
    low = (flat - high.astype(F32)).astype(BF16)
    split = jnp.concatenate([high, high, low], axis=1)
    return jnp.dot(split, down, preferred_element_type=F32).reshape(-1, GROUP, columns // 2)


def filtered_rows(rows, edges, wide, wide_grad, narrow):
    lane_tiles = wide.shape[2] // 128
    first, last = edges

    def tile_step(index, carry):
        lanes = pl.ds(pl.multiple_of(lax.rem(index, lane_tiles) * 128, 128), 128)
        subs = pl.ds(pl.multiple_of(lax.div(index, lane_tiles) * 8, 8), 8)

        def store(row, value):
            narrow[row, subs, lanes] = value

        load_grad = None if wide_grad is None else lambda row: wide_grad[row, subs, lanes]
        sinc_tile(rows, (first, last), lambda row: wide[row, subs, lanes], load_grad, store)
        return carry

    lax.fori_loop(0, GROUP // 8 * lane_tiles, tile_step, 0)


def fill_wide(rows, edges, raw, scale, shift, up, wide):
    spread = widened(raw, up) * scale
    wide[:RIM] = spread[:RIM] + shift * edges[0]
    wide[RIM : RIM + rows] = spread[RIM : RIM + rows] + shift
    wide[RIM + rows :] = spread[RIM + rows :] + shift * edges[1]


def forward_sinc_kernel(count, first_channel, me_ref, edge_ref, factors, up_sums, *refs):
    before, after, up_ref, down_ref = refs[:4]
    parts, (out, raw, up, down, out_rows, wide, narrow, sems) = refs[4 : 4 + count], refs[-8:]
    items, extent, width, columns = raw.shape
    rows = extent - 2 * RIM
    edges = edge_ref[0], edge_ref[1]
    own_channels = pl.ds(first_channel, width)
    pairs = row_blocks(me_ref[0], parts, raw, RIM, "mixed", first_channel)
    pairs += [
        (up_ref, up),
        (down_ref, down),
        (before.at[:, :, own_channels], raw.at[:, pl.ds(0, RIM)]),
        (after.at[:, :, own_channels], raw.at[:, pl.ds(RIM + rows, RIM)]),
    ]
    finished(started(sems, 0, pairs))
    leaving = []
    for item in range(items):
        for group in range(width // GROUP):
            at = slice(group * GROUP, (group + 1) * GROUP)
            shift = factors[items, at] * up_sums[...]
            fill_wide(rows, edges, raw[item, :, at], factors[item, at], shift, up[...], wide)
            filtered_rows(rows, edges, wide, None, narrow)
            result = narrowed(narrow[...], down[...])
            out_rows[at, item] = jnp.swapaxes(result, 0, 1).astype(BF16)
            target = out.at[pl.ds(first_channel + group * GROUP, GROUP), item]
            source = out_rows.at[pl.ds(group * GROUP, GROUP), item]
            leaving += started(sems, len(leaving), [(source, target)])
    finished(leaving)


def forward_sinc(me, edges, factors, tables, up_sums, before, after, parts, own, out, first_channel, earlier):
    count = len(parts)
    span, _, columns = parts[0].shape
    items, width = factors.shape[0] - 1, factors.shape[1]
    rows = span * count // items
    extent = rows + 2 * RIM
    return pl.pallas_call(
        functools.partial(forward_sinc_kernel, count, first_channel),
        out_shape=struct((own, items, rows, columns), BF16),
        in_specs=[IN_SMEM, IN_SMEM] + [IN_VMEM] * 2 + [IN_HBM] * (5 + count + len(out)),
        out_specs=IN_HBM,
        input_output_aliases={9 + count: 0} if out else {},
        scratch_shapes=[
            pltpu.VMEM((items, extent, width, columns), BF16),
            pltpu.VMEM(tables[0].shape, BF16),
            pltpu.VMEM(tables[1].shape, BF16),
            pltpu.VMEM((width, items, rows, columns), BF16),
            pltpu.VMEM((extent, GROUP, 2 * columns), F32),
            pltpu.VMEM((rows, GROUP, 2 * columns), F32),
            pltpu.SemaphoreType.DMA((max(count + 4, items * width // GROUP),)),
        ],
        compiler_params=PARAMS,
        name="forward_sinc",
    )(me, edges, factors, up_sums, before, after, *tables, *parts, earlier, *out)


def backward_sinc_kernel(count, first_channel, me_ref, edge_ref, factors, up_sums, *refs):
    before, after, cotangent, up_ref, down_ref = refs[:5]
    parts, (grad_bias, grad_demod) = refs[5 : 5 + count], refs[5 + count : 7 + count]
    grad_parts = refs[7 + count : 7 + 2 * count]
    raw, cot, up, down, grad_raw, wide, wide_grad, narrow, sems = refs[7 + 2 * count :]
    me = me_ref[0]
    items, extent, width, columns = raw.shape
    rows = extent - 2 * RIM
    edges = edge_ref[0], edge_ref[1]
    own_channels = pl.ds(first_channel, width)
    pairs = row_blocks(me, parts, raw, RIM, "mixed", first_channel)
    pairs += [
        (up_ref, up),
        (down_ref, down),
        (before.at[:, :, own_channels], raw.at[:, pl.ds(0, RIM)]),
        (after.at[:, :, own_channels], raw.at[:, pl.ds(RIM + rows, RIM)]),
        (cotangent.at[:, :, own_channels], cot),
    ]
    finished(started(sems, 0, pairs))
    for item in range(items):
        for group in range(width // GROUP):
            at = slice(group * GROUP, (group + 1) * GROUP)
            scale = factors[item, at]
            fill_wide(rows, edges, raw[item, :, at], scale, factors[items, at] * up_sums[...], up[...], wide)
            wide_grad[...] = widened(cot[item, :, at], up[...])
            filtered_rows(rows, edges, wide, wide_grad, narrow)
            grad = narrowed(narrow[...], down[...])
            scaled_grad = grad * scale
            grad_raw[item, 0, at] = (scaled_grad[0] * edges[0]).astype(BF16)
            grad_raw[item, 1 : rows + 1, at] = scaled_grad[1 : rows + 1].astype(BF16)
            grad_raw[item, rows + 1, at] = (scaled_grad[rows + 1] * edges[1]).astype(BF16)
            grad = grad[1 : rows + 1]
            own = raw[item, RIM : RIM + rows, at].astype(F32)
            grad_bias[item, at] = jnp.sum(jnp.sum(grad, axis=0), axis=1, keepdims=True)
            grad_demod[item, at] = jnp.sum(jnp.sum(grad * own, axis=0), axis=1, keepdims=True)
    blocks = count // items
    span = rows // blocks
    pairs = []
    kind = "near" if width < cotangent.shape[2] else "far"
    for x, part in zip(order(count, kind), grad_parts):
        dest = me ^ x
        pairs.append((grad_raw.at[dest // blocks, pl.ds((dest % blocks) * span, span + 2)], part))
    finished(started(sems, 0, pairs))


def backward_sinc(me, edges, factors, tables, up_sums, before, after, cotangent, parts, first_channel):
    count = len(parts)
    items, extent, _, columns = cotangent.shape
    span, width = parts[0].shape[0], factors.shape[1]
    rows = extent - 2 * RIM
    wide = pltpu.VMEM((extent, GROUP, 2 * columns), F32)
    outs = pl.pallas_call(
        functools.partial(backward_sinc_kernel, count, first_channel),
        out_shape=[struct((items, width, 1), F32)] * 2 + [struct((span + 2, width, columns), BF16)] * count,
        in_specs=[IN_SMEM, IN_SMEM] + [IN_VMEM] * 2 + [IN_HBM] * (5 + count),
        out_specs=[IN_VMEM, IN_VMEM] + [IN_HBM] * count,
        scratch_shapes=[
            pltpu.VMEM((items, extent, width, columns), BF16),
            pltpu.VMEM((items, extent, width, columns), BF16),
            pltpu.VMEM(tables[0].shape, BF16),
            pltpu.VMEM(tables[1].shape, BF16),
            pltpu.VMEM((items, rows + 2, width, columns), BF16),
            wide,
            wide,
            pltpu.VMEM((rows + 2, GROUP, 2 * columns), F32),
            pltpu.SemaphoreType.DMA((count + 5,)),
        ],
        compiler_params=PARAMS,
        name="backward_sinc",
    )(me, edges, factors, up_sums, before, after, cotangent, *tables, *parts)
    return outs[0], outs[1], outs[2:]


def scale_kernel(count, me_ref, scales, *refs):
    parts, (out, arrived, results, sems) = refs[:count], refs[count:]
    width, items, _, _ = out.shape
    finished(started(sems, 0, row_blocks(me_ref[0], parts, arrived, 0, "far")))
    leaving = []
    for item in range(items):
        for group in range(width // GROUP):
            at = slice(group * GROUP, (group + 1) * GROUP)
            value = arrived[item, :, at].astype(F32) * scales[item, at]
            results[at, item] = jnp.swapaxes(value, 0, 1)
            spot = pl.ds(group * GROUP, GROUP)
            leaving += started(sems, len(leaving), [(results.at[spot, item], out.at[spot, item])])
    finished(leaving)


def scaled(me, scales, parts, items):
    count = len(parts)
    span, width, columns = parts[0].shape
    rows = span * count // items
    return pl.pallas_call(
        functools.partial(scale_kernel, count),
        out_shape=struct((width, items, rows, columns), F32),
        in_specs=[IN_SMEM, IN_VMEM] + [IN_HBM] * count,
        out_specs=IN_HBM,
        scratch_shapes=[
            pltpu.VMEM((items, rows, width, columns), BF16),
            pltpu.VMEM((width, items, rows, columns), F32),
            pltpu.SemaphoreType.DMA((max(count, items * width // GROUP),)),
        ],
        compiler_params=PARAMS,
        name="scale_features",
    )(me, scales, *parts)


def in_thirds(value, lanes):
    terms = []
    for _ in range(3):
        terms.append(lax.reduce_precision(value, 8, 7))
        value = value - terms[-1]
    rows = jnp.stack(terms).astype(BF16).reshape(-1, lanes)
    return jnp.pad(rows, ((0, -rows.shape[0] % 16), (0, 0)))


def from_thirds(rows, shape):
    terms = rows.astype(F32).reshape(-1)[: 3 * shape[0] * shape[1]].reshape((3,) + shape)
    return terms[0] + terms[1] + terms[2]


def tree_sum(values):
    while len(values) > 1:
        values = [a + b for a, b in zip(values[::2], values[1::2])]
    return values[0]


def per_device(
    features,
    latent,
    affine,
    affine_bias,
    weight,
    out_bias,
    cotangent,
    latents_all,
    labels,
    class_means,
):
    highest = lax.Precision.HIGHEST
    own, items, rows, columns = features.shape
    channels = weight.shape[3]
    count = lax.axis_size("chan")
    dp_total = lax.axis_size("dp")
    me = lax.axis_index("chan")
    me_dp = lax.axis_index("dp")
    me_ref = me.astype(jnp.int32)[None]
    blocks = count // items
    span = rows // blocks
    split = max(1, min(2, own // GROUP))
    width = own // split

    styles = jnp.dot(latent, affine, preferred_element_type=F32) + affine_bias
    own_style = lax.dynamic_slice_in_dim(styles, me * own, own, 1)
    weight_full = weight.astype(F32)
    weight_sq = jnp.sum(weight_full * weight_full, axis=(0, 1))
    demod = lax.rsqrt(jnp.dot(styles * styles, weight_sq.T, precision=highest) + 1e-08)
    item = me // blocks
    item_scales = lax.dynamic_index_in_dim(styles, item, 0, keepdims=False).reshape(count, own, 1)

    before, after = from_neighbours(features, "dp", 2, 1)
    prepared = row_parts(me_ref, before, features, after, count)
    feats = exchange(prepared, "far")
    held, places = near_pieces(*weight_pieces(once(weight, prepared[0]), me_dp))
    shares = channels // held.shape[3]
    part = (me_dp % shares).astype(jnp.int32)[None]
    held = once(held, *feats[1:3], item_scales, demod)
    bit = shares // 2
    while bit > 1:
        met, met_places = met_pieces(held, places, bit)
        held, places = jnp.concatenate([held, met], axis=0), places + met_places
        bit //= 2
    cot_before, cot_after = from_neighbours(once(cotangent, feats[3]), "dp", 2, RIM)
    held = once(held, *feats[3:7])
    met, met_places = met_pieces(held, places, 1)
    pieces, places = [held, met], (tuple(places), tuple(met_places))

    table = up_table(columns)
    down_halves = halves(0.5 * table.T)
    tables = [np.concatenate(halves(table)), np.concatenate(down_halves + down_halves[:1])]
    up_sums = np.sum(table, axis=0)[None]
    edges = jnp.stack([me_dp > 0, me_dp < dp_total - 1]).astype(F32)

    item_scales = once(item_scales, cot_before, cot_after)
    raw_parts = conv_forward(me_ref, part, pieces, places, item_scales, feats)
    taps_backward = transposed_taps(
        me_ref, part, [once(piece, raw_parts[0]) for piece in pieces], places, channels
    )
    all_maps, grad_parts, bias_parts, demod_parts = [], [], [], []
    factors = jnp.concatenate([demod, out_bias[None]])[:, :, None]
    up = [(i, i + 1) for i in range(dp_total - 1)]
    down = [(j, i) for i, j in up]
    arrived = exchange(raw_parts, "mixed")
    cot = jnp.concatenate([cot_before, cotangent, cot_after], axis=2)
    cot = jnp.transpose(cot, (1, 2, 0, 3))
    head, tail = rims(me_ref, arrived, items, [taps_backward, cot])
    before, after = lax.ppermute(tail, "dp", up), lax.ppermute(head, "dp", down)
    for h in range(split):
        at = slice(h * width, (h + 1) * width)
        maps = (factors[:, at], tables, up_sums, before, after)
        all_maps.append(maps)
        bias_part, demod_part, parts = backward_sinc(
            me_ref, edges, *maps, cot, arrived, h * width
        )
        bias_parts.append(bias_part)
        demod_parts.append(demod_part)
        if h:
            parts = [once(part, *grad_parts[-4:]) for part in parts]
        grad_parts += exchange(parts, "near" if split > 1 else "far")
    bias_part = jnp.sum(jnp.concatenate(bias_parts, axis=1)[:, :, 0], axis=0)
    g_demod = jnp.concatenate(demod_parts, axis=1)[:, :, 0]

    output = [forward_sinc(me_ref, edges, *all_maps[0], arrived, own, [], 0, bias_parts[-1])]
    modded_parts, style_part, weight_sums = conv_backward(
        me_ref, item_scales, taps_backward, output[0], grad_parts, feats, dp_total
    )
    modded_parts = exchange(modded_parts, "far")
    for h in range(1, split):
        output = [forward_sinc(me_ref, edges, *all_maps[h], arrived, own, output, h * width, style_part)]
    output = output[0]
    grad_features = scaled(me_ref, own_style[:, :, None], modded_parts, items)

    grad_bias, g_demod_sum = lax.psum((once(bias_part, style_part), g_demod), "dp")
    cube = demod * demod * demod
    g_style_part = 2.0 * styles * jnp.dot(-0.5 * g_demod * cube, weight_sq, precision=highest)
    g_style_part = g_style_part + jnp.where(
        jnp.arange(items)[:, None] == item, style_part.reshape(1, channels), 0.0
    )
    g_wsq = jnp.dot((-0.5 * g_demod_sum * cube).T, styles * styles, precision=highest)

    tags = jnp.stack([labels // 64, labels % 64], axis=1).astype(BF16)
    tagged = jnp.concatenate([once(latents_all, head), jnp.pad(tags, ((0, 0), (0, 126)))], axis=1)
    tagged = lax.all_gather(tagged, ("dp", "chan"), axis=0, tiled=True)
    all_latents, tags = tagged[:, :-128], tagged[:, -128:-126].astype(F32)
    all_labels = (tags[:, 0] * 64.0 + tags[:, 1]).astype(jnp.int32)
    one_hot = all_labels[None, :] == jnp.arange(class_means.shape[0])[:, None]
    class_sums = jnp.dot(one_hot.astype(BF16), all_latents, preferred_element_type=F32)
    counts = jnp.sum(one_hot.astype(F32), axis=1)
    target = jnp.where(
        counts[:, None] > 0, class_sums / jnp.maximum(counts, 1.0)[:, None], class_means
    )

    share = channels // dp_total
    weight_sums = weight_sums.reshape(dp_total * 9 * channels, share)
    weight_sums = lax.psum_scatter(weight_sums, "dp", scatter_dimension=0, tiled=True)
    weight_sums = once(weight_sums.reshape(9, channels, share), *modded_parts, g_wsq, grad_bias, target, output)
    thirds = in_thirds(g_style_part, share)
    sent = []
    for x in order(count, "mixed"):
        part_x = lax.dynamic_slice_in_dim(weight_sums, (me ^ x) * own, own, 1)
        sent.append(jnp.concatenate([part_x.reshape(9 * own, share), thirds], axis=0))
    sent = exchange(sent, "mixed")
    g_weight = sum(value[: 9 * own].astype(F32) for value in sent).astype(BF16)
    style_sums = [from_thirds(value[9 * own :], styles.shape) for value in sent]
    g_style = tree_sum([style_sums[order(count, "mixed").index(x)] for x in range(count)])
    sent = once(jnp.concatenate([g_weight, in_thirds(g_style, share)], axis=0), grad_features)
    met = [sent] + [swapped(sent, "dp", x) for x in range(1, dp_total)]
    if share % 128 == 0:
        me_dp_ref = me_dp.astype(jnp.int32)[None]
        grad_weight = finished_weight(me_dp_ref, weight.reshape(9, own, channels), g_wsq, met)
    else:
        blocks = lax.all_gather(met[0][: 9 * own], "dp", axis=1, tiled=True)
        grad_weight = blocks.reshape(9, own, channels).astype(F32)
        grad_weight = grad_weight + 2.0 * weight_full.reshape(9, own, channels) * g_wsq
    grad_weight = grad_weight.reshape(weight.shape)
    g_style = tree_sum([from_thirds(value[9 * own :], styles.shape) for value in met])
    grad_affine_bias = jnp.sum(g_style, axis=0)
    grad_affine = jnp.dot(latent.astype(F32).T, g_style, precision=highest)
    grad_latent = jnp.dot(g_style, affine.astype(F32).T, precision=highest)
    return (
        output,
        grad_features,
        grad_latent,
        grad_affine,
        grad_affine_bias,
        grad_weight,
        grad_bias,
        target,
    )


def solution(mesh):
    in_specs = (
        P("chan", None, "dp", None),
        P(),
        P(),
        P(),
        P(None, None, "chan", None),
        P("chan"),
        P("chan", None, "dp", None),
        P(("dp", "chan"), None),
        P(("dp", "chan")),
        P(),
    )
    out_specs = (
        P("chan", None, "dp", None),
        P("chan", None, "dp", None),
        P(),
        P(),
        P(),
        P(None, None, "chan", None),
        P("chan"),
        P(),
    )
    return jax.shard_map(
        per_device, mesh=mesh, in_specs=in_specs, out_specs=out_specs, check_vma=False
    )
```

profile of v0, /device:TPU:0, one launch (start us, length us, event | category | flops | bytes accessed | tf_op | source)
XLA Modules:
  0.0 424.2 jit_solution(17446637404912548577)
XLA Ops:
  9.6 2.4 collective-permute-start
  14.1 3.2 collective-permute-done.1.after
  17.9 4.9 %row_parts.1 = (bf16[10,64,256]{2,1,0:T(8,128)(2,1)}, bf16[10,64,256]{2,1,0:T(8,128)(2,1)}, bf16[10,64,256]{2,1,0:T(8,128)(2,1)}, bf16[10,64,256]{2,1,0:T(8,128)...) custom-call(s32[1]{0:T(128)} %bitcast.me_ref, ...), custom_call_target="tpu_custom_call" | custom-call | tf_op jit(solution)/shard_map/row_parts/pallas_call | solution.py:114
  22.9 2.7 collective-permute-start.5
  25.7 5.3 %collective-permute-done.5 = bf16[1,9,64,128]{3,2,1,0:T(8,128)(2,1)S(1)} collective-permute-done((bf16[1,9,64,128]{3,2,1,0:T(8,128)(2,1)S(1)}, bf16[1,9,64,128]{3,2,1,0:T(8,128)(2,1)S(1)}, u32[]{:S(2)}, u32[]{:S(2)}) %collective-permute-start.5) | collective-permute-done | bytes 147488 | tf_op jit(solution)/shard_map/ppermute | solution.py:53
  33.6 2.2 collective-permute-start.10
  35.8 2.8 collective-permute-start.7
  39.7 14.5 %collective-permute-done.7 = bf16[2,9,64,128]{3,2,1,0:T(8,128)(2,1)S(1)} collective-permute-done((bf16[2,9,64,128]{3,2,1,0:T(8,128)(2,1)S(1)}, bf16[2,9,64,128]{3,2,1,0:T(8,128)(2,1)S(1)}, u32[]{:S(2)}, u32[]{:S(2)}) %collective-permute-start.7) | collective-permute-done | bytes 294944 | tf_op jit(solution)/shard_map/ppermute | solution.py:53
  54.2 6.3 %collective-permute-done.8 = bf16[2,9,64,128]{3,2,1,0:T(8,128)(2,1)S(1)} collective-permute-done((bf16[2,9,64,128]{3,2,1,0:T(8,128)(2,1)S(1)}, bf16[2,9,64,128]{3,2,1,0:T(8,128)(2,1)S(1)}, u32[]{:S(2)}, u32[]{:S(2)}) %collective-permute-start.8) | collective-permute-done | bytes 294944 | tf_op jit(solution)/shard_map/ppermute | solution.py:53
  60.5 3.7 collective-permute-done.10.refs_4_.refs_18_
  64.6 8.3 %collective-permute-start.2 = (bf16[10,64,256]{2,1,0:T(8,128)(2,1)}, bf16[10,64,256]{2,1,0:T(8,128)(2,1)S(1)}, u32[]{:S(2)}, u32[]{:S(2)}) collective-permute-start(bf16[10,64,256]{2,1,0:T(8,128)(2,1)} %get-tuple-element.75), channel_id=1, source_target_pairs={{0,6},{1,7},{2,4},{3,5},{4,2},{5,3},{6,0},{7,1},{8,14},{9,15},{10,... | collective-permute-start | bytes 983048 | tf_op jit(solution)/shard_map/ppermute | solution.py:53
  74.3 18.5 %collective-permute-done.11 = bf16[8,9,64,128]{3,2,1,0:T(8,128)(2,1)S(1)} collective-permute-done((bf16[8,9,64,128]{3,2,1,0:T(8,128)(2,1)S(1)}, bf16[8,9,64,128]{3,2,1,0:T(8,128)(2,1)S(1)}, u32[]{:S(2)}, u32[]{:S(2)}) %collective-permute-start.11) | collective-permute-done | bytes 1179680 | tf_op jit(solution)/shard_map/ppermute | solution.py:53
  95.0 2.9 collective-permute-start.3
  99.7 5.3 %collective-permute-start.16 = (bf16[10,64,256]{2,1,0:T(8,128)(2,1)}, bf16[10,64,256]{2,1,0:T(8,128)(2,1)S(1)}, u32[]{:S(2)}, u32[]{:S(2)}) collective-permute-start(bf16[10,64,256]{2,1,0:T(8,128)(2,1)} %get-tuple-element.87), channel_id=1, source_target_pairs={{0,3},{1,2},{2,1},{3,0},{4,7},{5,6},{6,5},{7,4},{8,11},{9,10},{10,... | collective-permute-start | bytes 983048 | tf_op jit(solution)/shard_map/ppermute | solution.py:53
  105.8 7.5 %collective-permute-done.16.refs_9_.refs_23_ = bf16[10,64,256]{2,1,0:T(8,128)(2,1)S(1)} collective-permute-done((bf16[10,64,256]{2,1,0:T(8,128)(2,1)}, bf16[10,64,256]{2,1,0:T(8,128)(2,1)S(1)}, u32[]{:S(2)}, u32[]{:S(2)}) %collective-permute-start.16) | collective-permute-done | bytes 327712 | tf_op jit(solution)/shard_map/ppermute | solution.py:53
  114.0 16.6 %conv_forward.1 = (bf16[8,64,256]{2,1,0:T(8,128)(2,1)}, bf16[8,64,256]{2,1,0:T(8,128)(2,1)}, bf16[8,64,256]{2,1,0:T(8,128)(2,1)}, bf16[8,64,256]{2,1,0:T(8,128)(...) custom-call(s32[1]{0:T(128)} %bitcast.me_ref, ...), custom_call_target="tpu_custom_call" | custom-call | tf_op jit(solution)/shard_map/conv_forward/pallas_call | solution.py:274
  130.6 4.4 %collective-permute-start.17 = (bf16[8,64,256]{2,1,0:T(8,128)(2,1)}, bf16[8,64,256]{2,1,0:T(8,128)(2,1)S(1)}, u32[]{:S(2)}, u32[]{:S(2)}) collective-permute-start(bf16[8,64,256]{2,1,0:T(8,128)(2,1)} %get-tuple-element.89), channel_id=1, source_target_pairs={{0,4},{1,5},{2,6},{3,7},{4,0},{5,1},{6,2},{7,3},{8,12},{9,13},{10,... | collective-permute-start | bytes 786440 | tf_op jit(solution)/shard_map/ppermute | solution.py:53
  135.6 2.8 copy.56
  141.1 2.6 collective-permute-start.21
  143.8 10.2 %collective-permute-done.17.refs_1_.refs_6_.refs_5_ = bf16[8,64,256]{2,1,0:T(8,128)(2,1)S(1)} collective-permute-done((bf16[8,64,256]{2,1,0:T(8,128)(2,1)}, bf16[8,64,256]{2,1,0:T(8,128)(2,1)S(1)}, u32[]{:S(2)}, u32[]{:S(2)}) %collective-permute-start.17) | collective-permute-done | bytes 262176 | tf_op jit(solution)/shard_map/ppermute | solution.py:53
  156.0 3.1 maximum_bitcast_fusion.refs_9_.refs_2_
  159.1 5.1 %transposed_taps.1.refs_8_.taps_ref = bf16[9,512,512]{2,1,0:T(8,128)(2,1)} custom-call(s32[1]{0:T(128)} %bitcast.me_ref, s32[1]{0:T(128)} %bitcast.5.part_ref, bf16[16,9,64,128]{3,2,1,0:T(8,128)(2,1)} %copy-done.1, bf16[16,9,64,128]{3,2,1,0:T(8,128)(2,1)} %collective-permute-done.15.refs_1_), custom_call_target="tpu_custom_call" | custom-call | tf_op jit(solution)/shard_map/transposed_taps/pallas_call | solution.py:177
  165.0 10.6 %collective-permute-done.22.refs_6_.refs_11_.refs_10_ = bf16[8,64,256]{2,1,0:T(8,128)(2,1)} collective-permute-done((bf16[8,64,256]{2,1,0:T(8,128)(2,1)}, bf16[8,64,256]{2,1,0:T(8,128)(2,1)}, u32[]{:S(2)}, u32[]{:S(2)}) %collective-permute-start.22) | collective-permute-done | bytes 262176 | tf_op jit(solution)/shard_map/ppermute | solution.py:53
  175.6 2.5 rims.1
  186.2 24.2 %backward_sinc.3 = (f32[2,32,1]{2,1,0:T(8,128)}, f32[2,32,1]{2,1,0:T(8,128)}, bf16[10,32,256]{2,1,0:T(8,128)(2,1)}, bf16[10,32,256]{2,1,0:T(8,128)(2,1)}, bf16[1...) custom-call(s32[1]{0:T(128)} %bitcast.me_ref, ...), custom_call_target="tpu_custom_call" | custom-call | tf_op jit(solution)/shard_map/backward_sinc/pallas_call | solution.py:648
  210.4 7.5 %collective-permute-start.29 = (bf16[10,32,256]{2,1,0:T(8,128)(2,1)}, bf16[10,32,256]{2,1,0:T(8,128)(2,1)S(1)}, u32[]{:S(2)}, u32[]{:S(2)}) collective-permute-start(bf16[10,32,256]{2,1,0:T(8,128)(2,1)} %get-tuple-element.105), channel_id=1, source_target_pairs={{0,4},{1,5},{2,6},{3,7},{4,0},{5,1},{6,2},{7,3},{8,12},{9,13},{10,... | collective-permute-start | bytes 491528 | tf_op jit(solution)/shard_map/ppermute | solution.py:53
  220.0 2.7 collective-permute-start.32
  224.0 24.3 %backward_sinc.2 = (f32[2,32,1]{2,1,0:T(8,128)}, f32[2,32,1]{2,1,0:T(8,128)}, bf16[10,32,256]{2,1,0:T(8,128)(2,1)}, bf16[10,32,256]{2,1,0:T(8,128)(2,1)}, bf16[1...) custom-call(s32[1]{0:T(128)} %bitcast.me_ref, ...), custom_call_target="tpu_custom_call" | custom-call | tf_op jit(solution)/shard_map/backward_sinc/pallas_call | solution.py:648
  252.0 3.8 collective-permute-start.34
  255.8 2.6 collective-permute-start.36
  264.8 15.3 %forward_sinc.2._.refs_13_ = bf16[64,2,32,256]{3,2,1,0:T(8,128)(2,1)} custom-call(s32[1]{0:T(128)} %bitcast.me_ref, f32[2]{0:T(128)} %add_convert_fusion.edge_ref, f32[3,32,1]{2,1,0:T(8,128)} %copy.67.factors, f32[1,512]{1,0:T(1,128)} %constant.99.clone.up_sums, bf16[2,7,64,256]{3,2,1,0:T(8,128)(2,1)} %copy-done.3, bf16[2,7,64,256]{3,2,1,0:T(8,128)(2,1)} %copy-done.4, ...), custom_call_target="tpu_custom_call" | custom-call | tf_op jit(solution)/shard_map/forward_sinc/pallas_call | solution.py:577
  281.5 28.2 %conv_backward.1 = (bf16[8,64,256]{2,1,0:T(8,128)(2,1)}, bf16[8,64,256]{2,1,0:T(8,128)(2,1)}, bf16[8,64,256]{2,1,0:T(8,128)(2,1)}, bf16[8,64,256]{2,1,0:T(8,128)...) custom-call(s32[1]{0:T(128)} %bitcast.me_ref, ...), custom_call_target="tpu_custom_call" | custom-call | tf_op jit(solution)/shard_map/conv_backward/pallas_call | solution.py:361
  311.0 6.2 %collective-permute-start.40 = (bf16[8,64,256]{2,1,0:T(8,128)(2,1)}, bf16[8,64,256]{2,1,0:T(8,128)(2,1)S(1)}, u32[]{:S(2)}, u32[]{:S(2)}) collective-permute-start(bf16[8,64,256]{2,1,0:T(8,128)(2,1)} %get-tuple-element.127), channel_id=1, source_target_pairs={{0,4},{1,5},{2,6},{3,7},{4,0},{5,1},{6,2},{7,3},{8,12},{9,13},{10,... | collective-permute-start | bytes 786440 | tf_op jit(solution)/shard_map/ppermute | solution.py:53
  317.2 2.5 collective-permute-start.41
  320.6 2.9 collective-permute-start.43
  325.5 15.6 %forward_sinc.3 = bf16[64,2,32,256]{3,2,1,0:T(8,128)(2,1)} custom-call(s32[1]{0:T(128)} %bitcast.me_ref, f32[2]{0:T(128)} %add_convert_fusion.edge_ref, f32[3,32,1]{2,1,0:T(8,128)} %copy.66.factors, f32[1,512]{1,0:T(1,128)} %constant.99.clone.up_sums, bf16[2,7,64,256]{3,2,1,0:T(8,128)(2,1)} %copy-done.3, ...), custom_call_target="tpu_custom_call", output_to_operand_aliasing={{}: (17, {})} | custom-call | tf_op jit(solution)/shard_map/forward_sinc/pallas_call | solution.py:577
  341.1 8.4 %all-reduce.3 = (f32[2,64]{1,0:T(2,128)S(1)}, f32[64]{0:T(128)}) all-reduce(f32[2,64]{1,0:T(2,128)S(1)} %maximum_bitcast_fusion.2, f32[64]{0:T(128)S(1)} %maximum_reduce_fusion), channel_id=1, replica_groups=mesh['dp'=4,'chan'=8] {'dp'}, use_global_device_ids=true, to_apply=%region_2.3 | all-reduce | flops 192 | bytes 1536 | tf_op jit(solution)/shard_map/psum | solution.py:819
  356.2 4.9 %divide_select_fusion = f32[1000,512]{1,0:T(8,128)} fusion(f32[1000,512]{1,0:T(8,128)} %param.22, bf16[2048,640]{1,0:T(8,128)(2,1)S(1)} %copy-done.47, s32[2048]{0:T(1024)S(1)} %fusion.8, f32[1000]{0:T(1024)S(1)} %broadcast_maximum_fusion, pred[1000]{0:T(1024)(128)(4,1)S(1)} %broadcast_compare_fusion), kind=kOutput, calls=%fused_computation.7 | convolution fusion | flops 2100224000 | bytes 6206464 | tf_op jit(solution)/shard_map/dot_general | solution.py:833
  362.6 4.9 %collective-permute-done.46.refs_7_ = bf16[8,64,256]{2,1,0:T(8,128)(2,1)S(1)} collective-permute-done((bf16[8,64,256]{2,1,0:T(8,128)(2,1)S(1)}, bf16[8,64,256]{2,1,0:T(8,128)(2,1)S(1)}, u32[]{:S(2)}, u32[]{:S(2)}) %collective-permute-start.46) | collective-permute-done | bytes 262176 | tf_op jit(solution)/shard_map/ppermute | solution.py:53
  369.2 2.4 collective-permute-start.53
  372.4 4.6 %scale_features.1 = f32[64,2,32,256]{3,2,1,0:T(8,128)} custom-call(s32[1]{0:T(128)} %bitcast.me_ref, f32[2,64,1]{2,1,0:T(8,128)} %copy.59.scales, bf16[8,64,256]{2,1,0:T(8,128)(2,1)} %get-tuple-element.126.refs_0_, bf16[8,64,256]{2,1,0:T(8,128)(2,1)} %copy-done.20, bf16[8,64,256]{2,1,0:T(8,128)(2,1)} %copy-done.21, bf16[8,64,256]{2,1,0:T(8,128)(2,1)} %copy-done.22, ...), custom_call_target="tpu_custom_call" | custom-call | tf_op jit(solution)/shard_map/scale_features/pallas_call | solution.py:689
  377.0 3.2 collective-permute-start.51
  383.9 2.1 collective-permute-start.50
  387.7 9.9 %collective-permute-done.49 = bf16[608,128]{1,0:T(8,128)(2,1)S(1)} collective-permute-done((bf16[608,128]{1,0:T(8,128)(2,1)S(1)}, bf16[608,128]{1,0:T(8,128)(2,1)S(1)}, u32[]{:S(2)}, u32[]{:S(2)}) %collective-permute-start.49) | collective-permute-done | bytes 155680 | tf_op jit(solution)/shard_map/ppermute | solution.py:53
  397.6 2.5 collective-permute-done.47
  402.4 4.4 %collective-permute-done.56.refs_3_ = bf16[608,128]{1,0:T(8,128)(2,1)S(1)} collective-permute-done((bf16[608,128]{1,0:T(8,128)(2,1)S(1)}, bf16[608,128]{1,0:T(8,128)(2,1)S(1)}, u32[]{:S(2)}, u32[]{:S(2)}) %collective-permute-start.56) | collective-permute-done | bytes 155680 | tf_op jit(solution)/shard_map/ppermute | solution.py:53
  406.8 2.5 collective-permute-done.55.refs_2_
  413.1 3.4 finished_weight.1
  (284 shorter events, 70.2 us)
Async XLA Ops:
  8.0 342.5 %all-gather.2.cloned.1.call-start = ((), (), s32[]{:S(2)}) async-start(), calls=%async_computation.2 | async-start | bytes 2703360 | tf_op jit(solution)/shard_map/all_gather | solution.py:829
  32.9 27.6 %collective-permute-start.9 = (bf16[10,64,256]{2,1,0:T(8,128)(2,1)}, bf16[10,64,256]{2,1,0:T(8,128)(2,1)S(1)}, u32[]{:S(2)}, u32[]{:S(2)}) collective-permute-start(bf16[10,64,256]{2,1,0:T(8,128)(2,1)} %get-tuple-element.80), channel_id=1, source_target_pairs={{0,4},{1,5},{2,6},{3,7},{4,0},{5,1},{6,2},{7,3},{8,12},{9,13},{10,... | collective-permute-start | bytes 983048 | tf_op jit(solution)/shard_map/ppermute | solution.py:53
  33.6 30.6 %collective-permute-start.10 = (bf16[10,64,256]{2,1,0:T(8,128)(2,1)}, bf16[10,64,256]{2,1,0:T(8,128)(2,1)S(1)}, u32[]{:S(2)}, u32[]{:S(2)}) collective-permute-start(bf16[10,64,256]{2,1,0:T(8,128)(2,1)} %get-tuple-element.81), channel_id=1, source_target_pairs={{0,5},{1,4},{2,7},{3,6},{4,1},{5,0},{6,3},{7,2},{8,13},{9,12},{10,... | collective-permute-start | bytes 983048 | tf_op jit(solution)/shard_map/ppermute | solution.py:53
  35.8 18.4 %collective-permute-start.7 = (bf16[2,9,64,128]{3,2,1,0:T(8,128)(2,1)S(1)}, bf16[2,9,64,128]{3,2,1,0:T(8,128)(2,1)S(1)}, u32[]{:S(2)}, u32[]{:S(2)}) collective-permute-start(bf16[2,9,64,128]{3,2,1,0:T(8,128)(2,1)S(1)} %pad_maximum_fusion.8), channel_id=1, source_target_pairs={{0,2},{1,3},{2,0},{3,1},{4,6},{5,7},{6,4},{7,5},{8,10},{9,11},{10,... | collective-permute-start | bytes 884744 | tf_op jit(solution)/shard_map/ppermute | solution.py:53
  38.6 21.9 %collective-permute-start.8 = (bf16[2,9,64,128]{3,2,1,0:T(8,128)(2,1)S(1)}, bf16[2,9,64,128]{3,2,1,0:T(8,128)(2,1)S(1)}, u32[]{:S(2)}, u32[]{:S(2)}) collective-permute-start(bf16[2,9,64,128]{3,2,1,0:T(8,128)(2,1)S(1)} %pad_maximum_fusion.8), channel_id=1, source_target_pairs={{0,3},{1,2},{2,1},{3,0},{4,7},{5,6},{6,5},{7,4},{8,11},{9,10},{10,... | collective-permute-start | bytes 884744 | tf_op jit(solution)/shard_map/ppermute | solution.py:53
  64.2 28.6 %collective-permute-start.11 = (bf16[8,9,64,128]{3,2,1,0:T(8,128)(2,1)S(1)}, bf16[8,9,64,128]{3,2,1,0:T(8,128)(2,1)S(1)}, u32[]{:S(2)}, u32[]{:S(2)}) collective-permute-start(bf16[8,9,64,128]{3,2,1,0:T(8,128)(2,1)S(1)} %constant_dynamic-update-slice_fusion), channel_id=1, source_target_pairs={{0,16},{8,24},{16,0},{24,8},{1,17},{9,25},{17,1},{25,9},{2,18},{10... | collective-permute-start | bytes 3538952 | tf_op jit(solution)/shard_map/ppermute | solution.py:53
  64.6 28.5 %collective-permute-start.2 = (bf16[10,64,256]{2,1,0:T(8,128)(2,1)}, bf16[10,64,256]{2,1,0:T(8,128)(2,1)S(1)}, u32[]{:S(2)}, u32[]{:S(2)}) collective-permute-start(bf16[10,64,256]{2,1,0:T(8,128)(2,1)} %get-tuple-element.75), channel_id=1, source_target_pairs={{0,6},{1,7},{2,4},{3,5},{4,2},{5,3},{6,0},{7,1},{8,14},{9,15},{10,... | collective-permute-start | bytes 983048 | tf_op jit(solution)/shard_map/ppermute | solution.py:53
  72.9 20.3 %collective-permute-start.12 = (bf16[10,64,256]{2,1,0:T(8,128)(2,1)}, bf16[10,64,256]{2,1,0:T(8,128)(2,1)S(1)}, u32[]{:S(2)}, u32[]{:S(2)}) collective-permute-start(bf16[10,64,256]{2,1,0:T(8,128)(2,1)} %get-tuple-element.83), channel_id=1, source_target_pairs={{0,7},{1,6},{2,5},{3,4},{4,3},{5,2},{6,1},{7,0},{8,15},{9,14},{10,... | collective-permute-start | bytes 983048 | tf_op jit(solution)/shard_map/ppermute | solution.py:53
  72.9 20.3 %collective-permute-start.13 = (bf16[10,64,256]{2,1,0:T(8,128)(2,1)}, bf16[10,64,256]{2,1,0:T(8,128)(2,1)S(1)}, u32[]{:S(2)}, u32[]{:S(2)}) collective-permute-start(bf16[10,64,256]{2,1,0:T(8,128)(2,1)} %get-tuple-element.84), channel_id=1, source_target_pairs={{0,1},{1,0},{2,3},{3,2},{4,5},{5,4},{6,7},{7,6},{8,9},{9,8},{10,11... | collective-permute-start | bytes 983048 | tf_op jit(solution)/shard_map/ppermute | solution.py:53
  74.3 18.8 %collective-permute-start.14 = (bf16[10,64,256]{2,1,0:T(8,128)(2,1)S(1)}, bf16[10,64,256]{2,1,0:T(8,128)(2,1)S(1)}, u32[]{:S(2)}, u32[]{:S(2)}) collective-permute-start(bf16[10,64,256]{2,1,0:T(8,128)(2,1)S(1)} %copy-done.54), channel_id=1, source_target_pairs={{0,2},{1,3},{2,0},{3,1},{4,6},{5,7},{6,4},{7,5},{8,10},{9,11},{10,... | collective-permute-start | bytes 983048 | tf_op jit(solution)/shard_map/ppermute | solution.py:53
  93.2 20.1 %collective-permute-start.15 = (bf16[16,9,64,128]{3,2,1,0:T(8,128)(2,1)S(1)}, bf16[16,9,64,128]{3,2,1,0:T(8,128)(2,1)}, u32[]{:S(2)}, u32[]{:S(2)}) collective-permute-start(bf16[16,9,64,128]{3,2,1,0:T(8,128)(2,1)S(1)} %pad_maximum_fusion.refs_0_), channel_id=1, source_target_pairs={{0,8},{8,0},{16,24},{24,16},{1,9},{9,1},{17,25},{25,17},{2,10},{10... | collective-permute-start | bytes 7077896 | tf_op jit(solution)/shard_map/ppermute | solution.py:53
  95.0 9.9 %collective-permute-start.3 = (bf16[64,2,7,256]{3,0,2,1:T(8,128)(2,1)S(1)}, bf16[64,2,7,256]{3,0,2,1:T(8,128)(2,1)}, u32[]{:S(2)}, u32[]{:S(2)}) collective-permute-start(bf16[64,2,7,256]{3,0,2,1:T(8,128)(2,1)S(1)} %get-tuple-element.177), channel_id=1, source_target_pairs={{0,8},{8,16},{16,24},{1,9},{9,17},{17,25},{2,10},{10,18},{18,26},{... | collective-permute-start | bytes 1376264 | tf_op jit(solution)/shard_map/ppermute | solution.py:49
  99.7 13.6 %collective-permute-start.16 = (bf16[10,64,256]{2,1,0:T(8,128)(2,1)}, bf16[10,64,256]{2,1,0:T(8,128)(2,1)S(1)}, u32[]{:S(2)}, u32[]{:S(2)}) collective-permute-start(bf16[10,64,256]{2,1,0:T(8,128)(2,1)} %get-tuple-element.87), channel_id=1, source_target_pairs={{0,3},{1,2},{2,1},{3,0},{4,7},{5,6},{6,5},{7,4},{8,11},{9,10},{10,... | collective-permute-start | bytes 983048 | tf_op jit(solution)/shard_map/ppermute | solution.py:53
  130.6 23.4 %collective-permute-start.17 = (bf16[8,64,256]{2,1,0:T(8,128)(2,1)}, bf16[8,64,256]{2,1,0:T(8,128)(2,1)S(1)}, u32[]{:S(2)}, u32[]{:S(2)}) collective-permute-start(bf16[8,64,256]{2,1,0:T(8,128)(2,1)} %get-tuple-element.89), channel_id=1, source_target_pairs={{0,4},{1,5},{2,6},{3,7},{4,0},{5,1},{6,2},{7,3},{8,12},{9,13},{10,... | collective-permute-start | bytes 786440 | tf_op jit(solution)/shard_map/ppermute | solution.py:53
  135.0 18.9 %collective-permute-start.18 = (bf16[8,64,256]{2,1,0:T(8,128)(2,1)}, bf16[8,64,256]{2,1,0:T(8,128)(2,1)S(1)}, u32[]{:S(2)}, u32[]{:S(2)}) collective-permute-start(bf16[8,64,256]{2,1,0:T(8,128)(2,1)} %get-tuple-element.90), channel_id=1, source_target_pairs={{0,1},{1,0},{2,3},{3,2},{4,5},{5,4},{6,7},{7,6},{8,9},{9,8},{10,11... | collective-permute-start | bytes 786440 | tf_op jit(solution)/shard_map/ppermute | solution.py:53
  138.3 26.7 %collective-permute-start.19 = (bf16[8,64,256]{2,1,0:T(8,128)(2,1)}, bf16[8,64,256]{2,1,0:T(8,128)(2,1)S(1)}, u32[]{:S(2)}, u32[]{:S(2)}) collective-permute-start(bf16[8,64,256]{2,1,0:T(8,128)(2,1)} %get-tuple-element.91), channel_id=1, source_target_pairs={{0,5},{1,4},{2,7},{3,6},{4,1},{5,0},{6,3},{7,2},{8,13},{9,12},{10,... | collective-permute-start | bytes 786440 | tf_op jit(solution)/shard_map/ppermute | solution.py:53
  139.5 25.6 %collective-permute-start.20 = (bf16[8,64,256]{2,1,0:T(8,128)(2,1)}, bf16[8,64,256]{2,1,0:T(8,128)(2,1)}, u32[]{:S(2)}, u32[]{:S(2)}) collective-permute-start(bf16[8,64,256]{2,1,0:T(8,128)(2,1)} %get-tuple-element.92), channel_id=1, source_target_pairs={{0,2},{1,3},{2,0},{3,1},{4,6},{5,7},{6,4},{7,5},{8,10},{9,11},{10,... | collective-permute-start | bytes 786440 | tf_op jit(solution)/shard_map/ppermute | solution.py:53
  141.1 23.9 %collective-permute-start.21 = (bf16[8,64,256]{2,1,0:T(8,128)(2,1)}, bf16[8,64,256]{2,1,0:T(8,128)(2,1)}, u32[]{:S(2)}, u32[]{:S(2)}) collective-permute-start(bf16[8,64,256]{2,1,0:T(8,128)(2,1)} %get-tuple-element.93), channel_id=1, source_target_pairs={{0,6},{1,7},{2,4},{3,5},{4,2},{5,3},{6,0},{7,1},{8,14},{9,15},{10,... | collective-permute-start | bytes 786440 | tf_op jit(solution)/shard_map/ppermute | solution.py:53
  154.0 21.6 %collective-permute-start.22 = (bf16[8,64,256]{2,1,0:T(8,128)(2,1)}, bf16[8,64,256]{2,1,0:T(8,128)(2,1)}, u32[]{:S(2)}, u32[]{:S(2)}) collective-permute-start(bf16[8,64,256]{2,1,0:T(8,128)(2,1)} %get-tuple-element.94), channel_id=1, source_target_pairs={{0,3},{1,2},{2,1},{3,0},{4,7},{5,6},{6,5},{7,4},{8,11},{9,10},{10,... | collective-permute-start | bytes 786440 | tf_op jit(solution)/shard_map/ppermute | solution.py:53
  154.0 21.6 %collective-permute-start.23 = (bf16[8,64,256]{2,1,0:T(8,128)(2,1)}, bf16[8,64,256]{2,1,0:T(8,128)(2,1)}, u32[]{:S(2)}, u32[]{:S(2)}) collective-permute-start(bf16[8,64,256]{2,1,0:T(8,128)(2,1)} %get-tuple-element.95), channel_id=1, source_target_pairs={{0,7},{1,6},{2,5},{3,4},{4,3},{5,2},{6,1},{7,0},{8,15},{9,14},{10,... | collective-permute-start | bytes 786440 | tf_op jit(solution)/shard_map/ppermute | solution.py:53
  178.8 188.7 %reduce-scatter.2.cloned.1.call-start = ((), (), s32[]{:S(2)}) async-start(), calls=%async_computation.1 | async-start | bytes 5898240 | tf_op jit(solution)/shard_map/reduce_scatter | solution.py:841
  210.4 37.8 %collective-permute-start.29 = (bf16[10,32,256]{2,1,0:T(8,128)(2,1)}, bf16[10,32,256]{2,1,0:T(8,128)(2,1)S(1)}, u32[]{:S(2)}, u32[]{:S(2)}) collective-permute-start(bf16[10,32,256]{2,1,0:T(8,128)(2,1)} %get-tuple-element.105), channel_id=1, source_target_pairs={{0,4},{1,5},{2,6},{3,7},{4,0},{5,1},{6,2},{7,3},{8,12},{9,13},{10,... | collective-permute-start | bytes 491528 | tf_op jit(solution)/shard_map/ppermute | solution.py:53
  217.9 31.5 %collective-permute-start.30 = (bf16[10,32,256]{2,1,0:T(8,128)(2,1)}, bf16[10,32,256]{2,1,0:T(8,128)(2,1)S(1)}, u32[]{:S(2)}, u32[]{:S(2)}) collective-permute-start(bf16[10,32,256]{2,1,0:T(8,128)(2,1)} %get-tuple-element.106), channel_id=1, source_target_pairs={{0,5},{1,4},{2,7},{3,6},{4,1},{5,0},{6,3},{7,2},{8,13},{9,12},{10,... | collective-permute-start | bytes 491528 | tf_op jit(solution)/shard_map/ppermute | solution.py:53
  218.0 33.4 %collective-permute-start.31 = (bf16[10,32,256]{2,1,0:T(8,128)(2,1)}, bf16[10,32,256]{2,1,0:T(8,128)(2,1)S(1)}, u32[]{:S(2)}, u32[]{:S(2)}) collective-permute-start(bf16[10,32,256]{2,1,0:T(8,128)(2,1)} %get-tuple-element.107), channel_id=1, source_target_pairs={{0,6},{1,7},{2,4},{3,5},{4,2},{5,3},{6,0},{7,1},{8,14},{9,15},{10,... | collective-permute-start | bytes 491528 | tf_op jit(solution)/shard_map/ppermute | solution.py:53
  220.0 31.3 %collective-permute-start.32 = (bf16[10,32,256]{2,1,0:T(8,128)(2,1)}, bf16[10,32,256]{2,1,0:T(8,128)(2,1)S(1)}, u32[]{:S(2)}, u32[]{:S(2)}) collective-permute-start(bf16[10,32,256]{2,1,0:T(8,128)(2,1)} %get-tuple-element.108), channel_id=1, source_target_pairs={{0,7},{1,6},{2,5},{3,4},{4,3},{5,2},{6,1},{7,0},{8,15},{9,14},{10,... | collective-permute-start | bytes 491528 | tf_op jit(solution)/shard_map/ppermute | solution.py:53
  223.4 32.4 %collective-permute-start.26 = (bf16[10,32,256]{2,1,0:T(8,128)(2,1)}, bf16[10,32,256]{2,1,0:T(8,128)(2,1)S(1)}, u32[]{:S(2)}, u32[]{:S(2)}) collective-permute-start(bf16[10,32,256]{2,1,0:T(8,128)(2,1)} %get-tuple-element.102), channel_id=1, source_target_pairs={{0,1},{1,0},{2,3},{3,2},{4,5},{5,4},{6,7},{7,6},{8,9},{9,8},{10,11... | collective-permute-start | bytes 491528 | tf_op jit(solution)/shard_map/ppermute | solution.py:53
  249.5 9.0 %collective-permute-start.28 = (bf16[10,32,256]{2,1,0:T(8,128)(2,1)S(1)}, bf16[10,32,256]{2,1,0:T(8,128)(2,1)S(1)}, u32[]{:S(2)}, u32[]{:S(2)}) collective-permute-start(bf16[10,32,256]{2,1,0:T(8,128)(2,1)S(1)} %copy-done.59), channel_id=1, source_target_pairs={{0,3},{1,2},{2,1},{3,0},{4,7},{5,6},{6,5},{7,4},{8,11},{9,10},{10,... | collective-permute-start | bytes 491528 | tf_op jit(solution)/shard_map/ppermute | solution.py:53
  252.0 10.8 %collective-permute-start.34 = (bf16[10,32,256]{2,1,0:T(8,128)(2,1)}, bf16[10,32,256]{2,1,0:T(8,128)(2,1)S(1)}, u32[]{:S(2)}, u32[]{:S(2)}) collective-permute-start(bf16[10,32,256]{2,1,0:T(8,128)(2,1)} %get-tuple-element.114), channel_id=1, source_target_pairs={{0,2},{1,3},{2,0},{3,1},{4,6},{5,7},{6,4},{7,5},{8,10},{9,11},{10,... | collective-permute-start | bytes 491528 | tf_op jit(solution)/shard_map/ppermute | solution.py:53
  255.8 24.5 %collective-permute-start.35 = (bf16[10,32,256]{2,1,0:T(8,128)(2,1)}, bf16[10,32,256]{2,1,0:T(8,128)(2,1)S(1)}, u32[]{:S(2)}, u32[]{:S(2)}) collective-permute-start(bf16[10,32,256]{2,1,0:T(8,128)(2,1)} %get-tuple-element.116), channel_id=1, source_target_pairs={{0,3},{1,2},{2,1},{3,0},{4,7},{5,6},{6,5},{7,4},{8,11},{9,10},{10,... | collective-permute-start | bytes 491528 | tf_op jit(solution)/shard_map/ppermute | solution.py:53
  255.8 24.4 %collective-permute-start.36 = (bf16[10,32,256]{2,1,0:T(8,128)(2,1)}, bf16[10,32,256]{2,1,0:T(8,128)(2,1)S(1)}, u32[]{:S(2)}, u32[]{:S(2)}) collective-permute-start(bf16[10,32,256]{2,1,0:T(8,128)(2,1)} %get-tuple-element.118), channel_id=1, source_target_pairs={{0,4},{1,5},{2,6},{3,7},{4,0},{5,1},{6,2},{7,3},{8,12},{9,13},{10,... | collective-permute-start | bytes 491528 | tf_op jit(solution)/shard_map/ppermute | solution.py:53
  258.5 21.8 %collective-permute-start.37 = (bf16[10,32,256]{2,1,0:T(8,128)(2,1)}, bf16[10,32,256]{2,1,0:T(8,128)(2,1)S(1)}, u32[]{:S(2)}, u32[]{:S(2)}) collective-permute-start(bf16[10,32,256]{2,1,0:T(8,128)(2,1)} %get-tuple-element.120), channel_id=1, source_target_pairs={{0,5},{1,4},{2,7},{3,6},{4,1},{5,0},{6,3},{7,2},{8,13},{9,12},{10,... | collective-permute-start | bytes 491528 | tf_op jit(solution)/shard_map/ppermute | solution.py:53
  259.7 20.6 %collective-permute-start.38 = (bf16[10,32,256]{2,1,0:T(8,128)(2,1)}, bf16[10,32,256]{2,1,0:T(8,128)(2,1)S(1)}, u32[]{:S(2)}, u32[]{:S(2)}) collective-permute-start(bf16[10,32,256]{2,1,0:T(8,128)(2,1)} %get-tuple-element.122), channel_id=1, source_target_pairs={{0,6},{1,7},{2,4},{3,5},{4,2},{5,3},{6,0},{7,1},{8,14},{9,15},{10,... | collective-permute-start | bytes 491528 | tf_op jit(solution)/shard_map/ppermute | solution.py:53
  262.8 18.0 %collective-permute-start.39 = (bf16[10,32,256]{2,1,0:T(8,128)(2,1)}, bf16[10,32,256]{2,1,0:T(8,128)(2,1)S(1)}, u32[]{:S(2)}, u32[]{:S(2)}) collective-permute-start(bf16[10,32,256]{2,1,0:T(8,128)(2,1)} %get-tuple-element.124), channel_id=1, source_target_pairs={{0,7},{1,6},{2,5},{3,4},{4,3},{5,2},{6,1},{7,0},{8,15},{9,14},{10,... | collective-permute-start | bytes 491528 | tf_op jit(solution)/shard_map/ppermute | solution.py:53
  311.0 42.3 %collective-permute-start.40 = (bf16[8,64,256]{2,1,0:T(8,128)(2,1)}, bf16[8,64,256]{2,1,0:T(8,128)(2,1)S(1)}, u32[]{:S(2)}, u32[]{:S(2)}) collective-permute-start(bf16[8,64,256]{2,1,0:T(8,128)(2,1)} %get-tuple-element.127), channel_id=1, source_target_pairs={{0,4},{1,5},{2,6},{3,7},{4,0},{5,1},{6,2},{7,3},{8,12},{9,13},{10,... | collective-permute-start | bytes 786440 | tf_op jit(solution)/shard_map/ppermute | solution.py:53
  317.2 36.9 %collective-permute-start.41 = (bf16[8,64,256]{2,1,0:T(8,128)(2,1)S(1)}, bf16[8,64,256]{2,1,0:T(8,128)(2,1)S(1)}, u32[]{:S(2)}, u32[]{:S(2)}) collective-permute-start(bf16[8,64,256]{2,1,0:T(8,128)(2,1)S(1)} %copy-done.58), channel_id=1, source_target_pairs={{0,5},{1,4},{2,7},{3,6},{4,1},{5,0},{6,3},{7,2},{8,13},{9,12},{10,... | collective-permute-start | bytes 786440 | tf_op jit(solution)/shard_map/ppermute | solution.py:53
  319.7 41.4 %collective-permute-start.42 = (bf16[8,64,256]{2,1,0:T(8,128)(2,1)}, bf16[8,64,256]{2,1,0:T(8,128)(2,1)S(1)}, u32[]{:S(2)}, u32[]{:S(2)}) collective-permute-start(bf16[8,64,256]{2,1,0:T(8,128)(2,1)} %get-tuple-element.129), channel_id=1, source_target_pairs={{0,6},{1,7},{2,4},{3,5},{4,2},{5,3},{6,0},{7,1},{8,14},{9,15},{10,... | collective-permute-start | bytes 786440 | tf_op jit(solution)/shard_map/ppermute | solution.py:53
  320.6 40.6 %collective-permute-start.43 = (bf16[8,64,256]{2,1,0:T(8,128)(2,1)}, bf16[8,64,256]{2,1,0:T(8,128)(2,1)S(1)}, u32[]{:S(2)}, u32[]{:S(2)}) collective-permute-start(bf16[8,64,256]{2,1,0:T(8,128)(2,1)} %get-tuple-element.130), channel_id=1, source_target_pairs={{0,7},{1,6},{2,5},{3,4},{4,3},{5,2},{6,1},{7,0},{8,15},{9,14},{10,... | collective-permute-start | bytes 786440 | tf_op jit(solution)/shard_map/ppermute | solution.py:53
  323.5 37.7 %collective-permute-start.44 = (bf16[8,64,256]{2,1,0:T(8,128)(2,1)S(1)}, bf16[8,64,256]{2,1,0:T(8,128)(2,1)S(1)}, u32[]{:S(2)}, u32[]{:S(2)}) collective-permute-start(bf16[8,64,256]{2,1,0:T(8,128)(2,1)S(1)} %copy-done.57), channel_id=1, source_target_pairs={{0,1},{1,0},{2,3},{3,2},{4,5},{5,4},{6,7},{7,6},{8,9},{9,8},{10,11... | collective-permute-start | bytes 786440 | tf_op jit(solution)/shard_map/ppermute | solution.py:53
  353.3 9.3 %collective-permute-start.45 = (bf16[8,64,256]{2,1,0:T(8,128)(2,1)S(1)}, bf16[8,64,256]{2,1,0:T(8,128)(2,1)S(1)}, u32[]{:S(2)}, u32[]{:S(2)}) collective-permute-start(bf16[8,64,256]{2,1,0:T(8,128)(2,1)S(1)} %copy-done.56), channel_id=1, source_target_pairs={{0,2},{1,3},{2,0},{3,1},{4,6},{5,7},{6,4},{7,5},{8,10},{9,11},{10,... | collective-permute-start | bytes 786440 | tf_op jit(solution)/shard_map/ppermute | solution.py:53
  354.1 13.4 %collective-permute-start.46 = (bf16[8,64,256]{2,1,0:T(8,128)(2,1)S(1)}, bf16[8,64,256]{2,1,0:T(8,128)(2,1)S(1)}, u32[]{:S(2)}, u32[]{:S(2)}) collective-permute-start(bf16[8,64,256]{2,1,0:T(8,128)(2,1)S(1)} %copy-done.55), channel_id=1, source_target_pairs={{0,3},{1,2},{2,1},{3,0},{4,7},{5,6},{6,5},{7,4},{8,11},{9,10},{10,... | collective-permute-start | bytes 786440 | tf_op jit(solution)/shard_map/ppermute | solution.py:53
  369.2 14.7 %collective-permute-start.53 = (bf16[608,128]{1,0:T(8,128)(2,1)S(1)}, bf16[608,128]{1,0:T(8,128)(2,1)S(1)}, u32[]{:S(2)}, u32[]{:S(2)}) collective-permute-start(bf16[608,128]{1,0:T(8,128)(2,1)S(1)} %get-tuple-element.193), channel_id=1, source_target_pairs={{0,7},{1,6},{2,5},{3,4},{4,3},{5,2},{6,1},{7,0},{8,15},{9,14},{10,... | collective-permute-start | bytes 466952 | tf_op jit(solution)/shard_map/ppermute | solution.py:53
  377.0 9.0 %collective-permute-start.51 = (bf16[608,128]{1,0:T(8,128)(2,1)S(1)}, bf16[608,128]{1,0:T(8,128)(2,1)S(1)}, u32[]{:S(2)}, u32[]{:S(2)}) collective-permute-start(bf16[608,128]{1,0:T(8,128)(2,1)S(1)} %get-tuple-element.191), channel_id=1, source_target_pairs={{0,6},{1,7},{2,4},{3,5},{4,2},{5,3},{6,0},{7,1},{8,14},{9,15},{10,... | collective-permute-start | bytes 466952 | tf_op jit(solution)/shard_map/ppermute | solution.py:53
  380.2 17.5 %collective-permute-start.49 = (bf16[608,128]{1,0:T(8,128)(2,1)S(1)}, bf16[608,128]{1,0:T(8,128)(2,1)S(1)}, u32[]{:S(2)}, u32[]{:S(2)}) collective-permute-start(bf16[608,128]{1,0:T(8,128)(2,1)S(1)} %get-tuple-element.189), channel_id=1, source_target_pairs={{0,5},{1,4},{2,7},{3,6},{4,1},{5,0},{6,3},{7,2},{8,13},{9,12},{10,... | collective-permute-start | bytes 466952 | tf_op jit(solution)/shard_map/ppermute | solution.py:53
  381.5 18.6 %collective-permute-start.47 = (bf16[608,128]{1,0:T(8,128)(2,1)S(1)}, bf16[608,128]{1,0:T(8,128)(2,1)S(1)}, u32[]{:S(2)}, u32[]{:S(2)}) collective-permute-start(bf16[608,128]{1,0:T(8,128)(2,1)S(1)} %get-tuple-element.194), channel_id=1, source_target_pairs={{0,4},{1,5},{2,6},{3,7},{4,0},{5,1},{6,2},{7,3},{8,12},{9,13},{10,... | collective-permute-start | bytes 466952 | tf_op jit(solution)/shard_map/ppermute | solution.py:53
  382.4 17.8 %collective-permute-start.52 = (bf16[608,128]{1,0:T(8,128)(2,1)S(1)}, bf16[608,128]{1,0:T(8,128)(2,1)S(1)}, u32[]{:S(2)}, u32[]{:S(2)}) collective-permute-start(bf16[608,128]{1,0:T(8,128)(2,1)S(1)} %get-tuple-element.192), channel_id=1, source_target_pairs={{0,3},{1,2},{2,1},{3,0},{4,7},{5,6},{6,5},{7,4},{8,11},{9,10},{10,... | collective-permute-start | bytes 466952 | tf_op jit(solution)/shard_map/ppermute | solution.py:53
  383.9 16.3 %collective-permute-start.50 = (bf16[608,128]{1,0:T(8,128)(2,1)S(1)}, bf16[608,128]{1,0:T(8,128)(2,1)S(1)}, u32[]{:S(2)}, u32[]{:S(2)}) collective-permute-start(bf16[608,128]{1,0:T(8,128)(2,1)S(1)} %get-tuple-element.190), channel_id=1, source_target_pairs={{0,2},{1,3},{2,0},{3,1},{4,6},{5,7},{6,4},{7,5},{8,10},{9,11},{10,... | collective-permute-start | bytes 466952 | tf_op jit(solution)/shard_map/ppermute | solution.py:53
  386.0 14.2 %collective-permute-start.48 = (bf16[608,128]{1,0:T(8,128)(2,1)S(1)}, bf16[608,128]{1,0:T(8,128)(2,1)S(1)}, u32[]{:S(2)}, u32[]{:S(2)}) collective-permute-start(bf16[608,128]{1,0:T(8,128)(2,1)S(1)} %get-tuple-element.188), channel_id=1, source_target_pairs={{0,1},{1,0},{2,3},{3,2},{4,5},{5,4},{6,7},{7,6},{8,9},{9,8},{10,11... | collective-permute-start | bytes 466952 | tf_op jit(solution)/shard_map/ppermute | solution.py:53
  400.6 8.7 %collective-permute-start.55 = (bf16[608,128]{1,0:T(8,128)(2,1)S(1)}, bf16[608,128]{1,0:T(8,128)(2,1)S(1)}, u32[]{:S(2)}, u32[]{:S(2)}) collective-permute-start(bf16[608,128]{1,0:T(8,128)(2,1)S(1)} %fusion.18.refs_0_), channel_id=1, source_target_pairs={{0,16},{8,24},{16,0},{24,8},{1,17},{9,25},{17,1},{25,9},{2,18},{10... | collective-permute-start | bytes 466952 | tf_op jit(solution)/shard_map/ppermute | solution.py:53
  (73 other events, 779.8 us)
Sparse Core Ops, SparseCore 0:
  178.9 70.0 all-gather.1
Sparse Core Ops, SparseCore 1:
  309.9 54.9 reduce-scatter.1
where the time goes:
time: 429 us; the launch traced here: 424 us
  Pallas kernels  145 us (34%)
  waiting for transfers between devices  111 us (26%)
  starting transfers between devices  109 us (25%)
  between operations  16.8 us (4%)
  local copies, waits for them, and re-layouts  16.3 us (4%)
  other arithmetic  8.86 us (2%)
  matrix products  8.82 us (2%)
  blocking collectives  8.38 us (2%)
    ppermute x51, waiting for transfers between devices, swapped(): lax.ppermute(value, axis, [(i, i ^ bits) for i in range(lax.axis_size(axi...  106 us
    ppermute x51, starting transfers between devices, swapped(): lax.ppermute(value, axis, [(i, i ^ bits) for i in range(lax.axis_size(axi...  97.7 us
    pallas_call x2, Pallas kernels, backward_sinc(): pl.pallas_call(functools.partial(backward_sinc_kernel, count, first_chann...  48.5 us
    pallas_call x2, Pallas kernels, forward_sinc(): pl.pallas_call(functools.partial(forward_sinc_kernel, count, first_channe...  30.9 us
    pallas_call x1, Pallas kernels, conv_backward(): pl.pallas_call(functools.partial(backward_kernel, count, split), out_shap...  28.2 us
    pallas_call x1, Pallas kernels, conv_forward(): pl.pallas_call(functools.partial(forward_kernel, count, places), out_shap...  16.6 us
    unnamed x133, local copies, waits for them, and re-layouts  9.65 us
  transfers between devices with their start and end apart: 59, of which 20 were waited for; matrix products, arithmetic and copies ran while one was open for 5% of the time, Pallas kernels for 28%

commit v1 on v0

--- a/solution.py
+++ b/solution.py
@@ -220,7 +220,7 @@
             shifted[row, 2, source] = after.astype(BF16)
         return carry
 
-    lax.fori_loop(0, rows, row_step, 0)
+    lax.fori_loop(0, rows, row_step, 0, unroll=2)
 
 
 def convolved(taps, shifted, row, channels, columns):

time: 429 us -> 429 us (level)
  no operation moved by 1% of the time
where the time goes in v1:
time: 429 us; the launch traced here: 424 us
  Pallas kernels  145 us (34%)
  waiting for transfers between devices  111 us (26%)
  starting transfers between devices  109 us (25%)
  between operations  16.8 us (4%)
  local copies, waits for them, and re-layouts  16.3 us (4%)
  other arithmetic  8.86 us (2%)
  matrix products  8.83 us (2%)
  blocking collectives  8.39 us (2%)
    ppermute x51, waiting for transfers between devices, swapped(): lax.ppermute(value, axis, [(i, i ^ bits) for i in range(lax.axis_size(axi...  106 us
    ppermute x51, starting transfers between devices, swapped(): lax.ppermute(value, axis, [(i, i ^ bits) for i in range(lax.axis_size(axi...  97.7 us
    pallas_call x2, Pallas kernels, backward_sinc(): pl.pallas_call(functools.partial(backward_sinc_kernel, count, first_chann...  48.5 us
    pallas_call x2, Pallas kernels, forward_sinc(): pl.pallas_call(functools.partial(forward_sinc_kernel, count, first_channe...  30.9 us
    pallas_call x1, Pallas kernels, conv_backward(): pl.pallas_call(functools.partial(backward_kernel, count, split), out_shap...  28.2 us
    pallas_call x1, Pallas kernels, conv_forward(): pl.pallas_call(functools.partial(forward_kernel, count, places), out_shap...  16.3 us
    unnamed x133, local copies, waits for them, and re-layouts  9.65 us
  transfers between devices with their start and end apart: 59, of which 20 were waited for; matrix products, arithmetic and copies ran while one was open for 5% of the time, Pallas kernels for 28%

profile of v1, /device:TPU:0, one launch (start us, length us, event | category | flops | bytes accessed | tf_op | source)
XLA Modules:
  0.0 423.9 jit_solution(16719563734191216013)
XLA Ops:
  9.6 2.4 collective-permute-start
  14.1 3.2 collective-permute-done.1.after
  17.9 4.9 %row_parts.1 = (bf16[10,64,256]{2,1,0:T(8,128)(2,1)}, bf16[10,64,256]{2,1,0:T(8,128)(2,1)}, bf16[10,64,256]{2,1,0:T(8,128)(2,1)}, bf16[10,64,256]{2,1,0:T(8,128)...) custom-call(s32[1]{0:T(128)} %bitcast.me_ref, ...), custom_call_target="tpu_custom_call" | custom-call | tf_op jit(solution)/shard_map/row_parts/pallas_call | solution.py:114
  22.9 2.7 collective-permute-start.5
  25.7 5.3 %collective-permute-done.5 = bf16[1,9,64,128]{3,2,1,0:T(8,128)(2,1)S(1)} collective-permute-done((bf16[1,9,64,128]{3,2,1,0:T(8,128)(2,1)S(1)}, bf16[1,9,64,128]{3,2,1,0:T(8,128)(2,1)S(1)}, u32[]{:S(2)}, u32[]{:S(2)}) %collective-permute-start.5) | collective-permute-done | bytes 147488 | tf_op jit(solution)/shard_map/ppermute | solution.py:53
  33.6 2.2 collective-permute-start.10
  35.8 2.8 collective-permute-start.7
  39.7 14.5 %collective-permute-done.7 = bf16[2,9,64,128]{3,2,1,0:T(8,128)(2,1)S(1)} collective-permute-done((bf16[2,9,64,128]{3,2,1,0:T(8,128)(2,1)S(1)}, bf16[2,9,64,128]{3,2,1,0:T(8,128)(2,1)S(1)}, u32[]{:S(2)}, u32[]{:S(2)}) %collective-permute-start.7) | collective-permute-done | bytes 294944 | tf_op jit(solution)/shard_map/ppermute | solution.py:53
  54.2 6.3 %collective-permute-done.8 = bf16[2,9,64,128]{3,2,1,0:T(8,128)(2,1)S(1)} collective-permute-done((bf16[2,9,64,128]{3,2,1,0:T(8,128)(2,1)S(1)}, bf16[2,9,64,128]{3,2,1,0:T(8,128)(2,1)S(1)}, u32[]{:S(2)}, u32[]{:S(2)}) %collective-permute-start.8) | collective-permute-done | bytes 294944 | tf_op jit(solution)/shard_map/ppermute | solution.py:53
  60.5 3.7 collective-permute-done.10.refs_4_.refs_18_
  64.6 8.3 %collective-permute-start.2 = (bf16[10,64,256]{2,1,0:T(8,128)(2,1)}, bf16[10,64,256]{2,1,0:T(8,128)(2,1)S(1)}, u32[]{:S(2)}, u32[]{:S(2)}) collective-permute-start(bf16[10,64,256]{2,1,0:T(8,128)(2,1)} %get-tuple-element.75), channel_id=1, source_target_pairs={{0,6},{1,7},{2,4},{3,5},{4,2},{5,3},{6,0},{7,1},{8,14},{9,15},{10,... | collective-permute-start | bytes 983048 | tf_op jit(solution)/shard_map/ppermute | solution.py:53
  74.3 18.5 %collective-permute-done.11 = bf16[8,9,64,128]{3,2,1,0:T(8,128)(2,1)S(1)} collective-permute-done((bf16[8,9,64,128]{3,2,1,0:T(8,128)(2,1)S(1)}, bf16[8,9,64,128]{3,2,1,0:T(8,128)(2,1)S(1)}, u32[]{:S(2)}, u32[]{:S(2)}) %collective-permute-start.11) | collective-permute-done | bytes 1179680 | tf_op jit(solution)/shard_map/ppermute | solution.py:53
  95.0 2.9 collective-permute-start.3
  99.7 5.3 %collective-permute-start.16 = (bf16[10,64,256]{2,1,0:T(8,128)(2,1)}, bf16[10,64,256]{2,1,0:T(8,128)(2,1)S(1)}, u32[]{:S(2)}, u32[]{:S(2)}) collective-permute-start(bf16[10,64,256]{2,1,0:T(8,128)(2,1)} %get-tuple-element.87), channel_id=1, source_target_pairs={{0,3},{1,2},{2,1},{3,0},{4,7},{5,6},{6,5},{7,4},{8,11},{9,10},{10,... | collective-permute-start | bytes 983048 | tf_op jit(solution)/shard_map/ppermute | solution.py:53
  105.8 7.5 %collective-permute-done.16.refs_9_.refs_23_ = bf16[10,64,256]{2,1,0:T(8,128)(2,1)S(1)} collective-permute-done((bf16[10,64,256]{2,1,0:T(8,128)(2,1)}, bf16[10,64,256]{2,1,0:T(8,128)(2,1)S(1)}, u32[]{:S(2)}, u32[]{:S(2)}) %collective-permute-start.16) | collective-permute-done | bytes 327712 | tf_op jit(solution)/shard_map/ppermute | solution.py:53
  114.0 16.3 %conv_forward.1 = (bf16[8,64,256]{2,1,0:T(8,128)(2,1)}, bf16[8,64,256]{2,1,0:T(8,128)(2,1)}, bf16[8,64,256]{2,1,0:T(8,128)(2,1)}, bf16[8,64,256]{2,1,0:T(8,128)(...) custom-call(s32[1]{0:T(128)} %bitcast.me_ref, ...), custom_call_target="tpu_custom_call" | custom-call | tf_op jit(solution)/shard_map/conv_forward/pallas_call | solution.py:274
  130.3 4.4 %collective-permute-start.17 = (bf16[8,64,256]{2,1,0:T(8,128)(2,1)}, bf16[8,64,256]{2,1,0:T(8,128)(2,1)S(1)}, u32[]{:S(2)}, u32[]{:S(2)}) collective-permute-start(bf16[8,64,256]{2,1,0:T(8,128)(2,1)} %get-tuple-element.89), channel_id=1, source_target_pairs={{0,4},{1,5},{2,6},{3,7},{4,0},{5,1},{6,2},{7,3},{8,12},{9,13},{10,... | collective-permute-start | bytes 786440 | tf_op jit(solution)/shard_map/ppermute | solution.py:53
  135.3 2.8 copy.56
  140.8 2.6 collective-permute-start.21
  143.5 10.2 %collective-permute-done.17.refs_1_.refs_6_.refs_5_ = bf16[8,64,256]{2,1,0:T(8,128)(2,1)S(1)} collective-permute-done((bf16[8,64,256]{2,1,0:T(8,128)(2,1)}, bf16[8,64,256]{2,1,0:T(8,128)(2,1)S(1)}, u32[]{:S(2)}, u32[]{:S(2)}) %collective-permute-start.17) | collective-permute-done | bytes 262176 | tf_op jit(solution)/shard_map/ppermute | solution.py:53
  155.7 3.1 maximum_bitcast_fusion.refs_9_.refs_2_
  158.8 5.1 %transposed_taps.1.refs_8_.taps_ref = bf16[9,512,512]{2,1,0:T(8,128)(2,1)} custom-call(s32[1]{0:T(128)} %bitcast.me_ref, s32[1]{0:T(128)} %bitcast.5.part_ref, bf16[16,9,64,128]{3,2,1,0:T(8,128)(2,1)} %copy-done.1, bf16[16,9,64,128]{3,2,1,0:T(8,128)(2,1)} %collective-permute-done.15.refs_1_), custom_call_target="tpu_custom_call" | custom-call | tf_op jit(solution)/shard_map/transposed_taps/pallas_call | solution.py:177
  164.8 10.6 %collective-permute-done.22.refs_6_.refs_11_.refs_10_ = bf16[8,64,256]{2,1,0:T(8,128)(2,1)} collective-permute-done((bf16[8,64,256]{2,1,0:T(8,128)(2,1)}, bf16[8,64,256]{2,1,0:T(8,128)(2,1)}, u32[]{:S(2)}, u32[]{:S(2)}) %collective-permute-start.22) | collective-permute-done | bytes 262176 | tf_op jit(solution)/shard_map/ppermute | solution.py:53
  175.3 2.5 rims.1
  186.0 24.2 %backward_sinc.3 = (f32[2,32,1]{2,1,0:T(8,128)}, f32[2,32,1]{2,1,0:T(8,128)}, bf16[10,32,256]{2,1,0:T(8,128)(2,1)}, bf16[10,32,256]{2,1,0:T(8,128)(2,1)}, bf16[1...) custom-call(s32[1]{0:T(128)} %bitcast.me_ref, ...), custom_call_target="tpu_custom_call" | custom-call | tf_op jit(solution)/shard_map/backward_sinc/pallas_call | solution.py:648
  210.2 7.5 %collective-permute-start.29 = (bf16[10,32,256]{2,1,0:T(8,128)(2,1)}, bf16[10,32,256]{2,1,0:T(8,128)(2,1)S(1)}, u32[]{:S(2)}, u32[]{:S(2)}) collective-permute-start(bf16[10,32,256]{2,1,0:T(8,128)(2,1)} %get-tuple-element.105), channel_id=1, source_target_pairs={{0,4},{1,5},{2,6},{3,7},{4,0},{5,1},{6,2},{7,3},{8,12},{9,13},{10,... | collective-permute-start | bytes 491528 | tf_op jit(solution)/shard_map/ppermute | solution.py:53
  219.8 2.7 collective-permute-start.32
  223.7 24.3 %backward_sinc.2 = (f32[2,32,1]{2,1,0:T(8,128)}, f32[2,32,1]{2,1,0:T(8,128)}, bf16[10,32,256]{2,1,0:T(8,128)(2,1)}, bf16[10,32,256]{2,1,0:T(8,128)(2,1)}, bf16[1...) custom-call(s32[1]{0:T(128)} %bitcast.me_ref, ...), custom_call_target="tpu_custom_call" | custom-call | tf_op jit(solution)/shard_map/backward_sinc/pallas_call | solution.py:648
  251.7 3.8 collective-permute-start.34
  255.6 2.6 collective-permute-start.36
  264.5 15.3 %forward_sinc.2._.refs_13_ = bf16[64,2,32,256]{3,2,1,0:T(8,128)(2,1)} custom-call(s32[1]{0:T(128)} %bitcast.me_ref, f32[2]{0:T(128)} %add_convert_fusion.edge_ref, f32[3,32,1]{2,1,0:T(8,128)} %copy.67.factors, f32[1,512]{1,0:T(1,128)} %constant.99.clone.up_sums, bf16[2,7,64,256]{3,2,1,0:T(8,128)(2,1)} %copy-done.3, bf16[2,7,64,256]{3,2,1,0:T(8,128)(2,1)} %copy-done.4, ...), custom_call_target="tpu_custom_call" | custom-call | tf_op jit(solution)/shard_map/forward_sinc/pallas_call | solution.py:577
  281.2 28.2 %conv_backward.1 = (bf16[8,64,256]{2,1,0:T(8,128)(2,1)}, bf16[8,64,256]{2,1,0:T(8,128)(2,1)}, bf16[8,64,256]{2,1,0:T(8,128)(2,1)}, bf16[8,64,256]{2,1,0:T(8,128)...) custom-call(s32[1]{0:T(128)} %bitcast.me_ref, ...), custom_call_target="tpu_custom_call" | custom-call | tf_op jit(solution)/shard_map/conv_backward/pallas_call | solution.py:361
  310.7 6.2 %collective-permute-start.40 = (bf16[8,64,256]{2,1,0:T(8,128)(2,1)}, bf16[8,64,256]{2,1,0:T(8,128)(2,1)S(1)}, u32[]{:S(2)}, u32[]{:S(2)}) collective-permute-start(bf16[8,64,256]{2,1,0:T(8,128)(2,1)} %get-tuple-element.127), channel_id=1, source_target_pairs={{0,4},{1,5},{2,6},{3,7},{4,0},{5,1},{6,2},{7,3},{8,12},{9,13},{10,... | collective-permute-start | bytes 786440 | tf_op jit(solution)/shard_map/ppermute | solution.py:53
  316.9 2.5 collective-permute-start.41
  320.3 2.9 collective-permute-start.43
  325.2 15.6 %forward_sinc.3 = bf16[64,2,32,256]{3,2,1,0:T(8,128)(2,1)} custom-call(s32[1]{0:T(128)} %bitcast.me_ref, f32[2]{0:T(128)} %add_convert_fusion.edge_ref, f32[3,32,1]{2,1,0:T(8,128)} %copy.66.factors, f32[1,512]{1,0:T(1,128)} %constant.99.clone.up_sums, bf16[2,7,64,256]{3,2,1,0:T(8,128)(2,1)} %copy-done.3, ...), custom_call_target="tpu_custom_call", output_to_operand_aliasing={{}: (17, {})} | custom-call | tf_op jit(solution)/shard_map/forward_sinc/pallas_call | solution.py:577
  340.8 8.4 %all-reduce.3 = (f32[2,64]{1,0:T(2,128)S(1)}, f32[64]{0:T(128)}) all-reduce(f32[2,64]{1,0:T(2,128)S(1)} %maximum_bitcast_fusion.2, f32[64]{0:T(128)S(1)} %maximum_reduce_fusion), channel_id=1, replica_groups=mesh['dp'=4,'chan'=8] {'dp'}, use_global_device_ids=true, to_apply=%region_2.3 | all-reduce | flops 192 | bytes 1536 | tf_op jit(solution)/shard_map/psum | solution.py:819
  353.8 2.1 collective-permute-start.46
  355.9 4.9 %divide_select_fusion = f32[1000,512]{1,0:T(8,128)} fusion(f32[1000,512]{1,0:T(8,128)} %param.22, bf16[2048,640]{1,0:T(8,128)(2,1)S(1)} %copy-done.47, s32[2048]{0:T(1024)S(1)} %fusion.8, f32[1000]{0:T(1024)S(1)} %broadcast_maximum_fusion, pred[1000]{0:T(1024)(128)(4,1)S(1)} %broadcast_compare_fusion), kind=kOutput, calls=%fused_computation.7 | convolution fusion | flops 2100224000 | bytes 6206464 | tf_op jit(solution)/shard_map/dot_general | solution.py:833
  362.3 4.9 %collective-permute-done.46.refs_7_ = bf16[8,64,256]{2,1,0:T(8,128)(2,1)S(1)} collective-permute-done((bf16[8,64,256]{2,1,0:T(8,128)(2,1)S(1)}, bf16[8,64,256]{2,1,0:T(8,128)(2,1)S(1)}, u32[]{:S(2)}, u32[]{:S(2)}) %collective-permute-start.46) | collective-permute-done | bytes 262176 | tf_op jit(solution)/shard_map/ppermute | solution.py:53
  368.9 2.4 collective-permute-start.53
  372.1 4.6 %scale_features.1 = f32[64,2,32,256]{3,2,1,0:T(8,128)} custom-call(s32[1]{0:T(128)} %bitcast.me_ref, f32[2,64,1]{2,1,0:T(8,128)} %copy.59.scales, bf16[8,64,256]{2,1,0:T(8,128)(2,1)} %get-tuple-element.126.refs_0_, bf16[8,64,256]{2,1,0:T(8,128)(2,1)} %copy-done.20, bf16[8,64,256]{2,1,0:T(8,128)(2,1)} %copy-done.21, bf16[8,64,256]{2,1,0:T(8,128)(2,1)} %copy-done.22, ...), custom_call_target="tpu_custom_call" | custom-call | tf_op jit(solution)/shard_map/scale_features/pallas_call | solution.py:689
  376.7 3.1 collective-permute-start.51
  387.4 9.9 %collective-permute-done.49 = bf16[608,128]{1,0:T(8,128)(2,1)S(1)} collective-permute-done((bf16[608,128]{1,0:T(8,128)(2,1)S(1)}, bf16[608,128]{1,0:T(8,128)(2,1)S(1)}, u32[]{:S(2)}, u32[]{:S(2)}) %collective-permute-start.49) | collective-permute-done | bytes 155680 | tf_op jit(solution)/shard_map/ppermute | solution.py:53
  397.3 2.5 collective-permute-done.47
  402.1 4.4 %collective-permute-done.56.refs_3_ = bf16[608,128]{1,0:T(8,128)(2,1)S(1)} collective-permute-done((bf16[608,128]{1,0:T(8,128)(2,1)S(1)}, bf16[608,128]{1,0:T(8,128)(2,1)S(1)}, u32[]{:S(2)}, u32[]{:S(2)}) %collective-permute-start.56) | collective-permute-done | bytes 155680 | tf_op jit(solution)/shard_map/ppermute | solution.py:53
  406.5 2.5 collective-permute-done.55.refs_2_
  412.8 3.4 finished_weight.1
  (284 shorter events, 70.3 us)
Async XLA Ops:
  8.0 342.2 %all-gather.2.cloned.1.call-start = ((), (), s32[]{:S(2)}) async-start(), calls=%async_computation.2 | async-start | bytes 2703360 | tf_op jit(solution)/shard_map/all_gather | solution.py:829
  32.9 27.6 %collective-permute-start.9 = (bf16[10,64,256]{2,1,0:T(8,128)(2,1)}, bf16[10,64,256]{2,1,0:T(8,128)(2,1)S(1)}, u32[]{:S(2)}, u32[]{:S(2)}) collective-permute-start(bf16[10,64,256]{2,1,0:T(8,128)(2,1)} %get-tuple-element.80), channel_id=1, source_target_pairs={{0,4},{1,5},{2,6},{3,7},{4,0},{5,1},{6,2},{7,3},{8,12},{9,13},{10,... | collective-permute-start | bytes 983048 | tf_op jit(solution)/shard_map/ppermute | solution.py:53
  33.6 30.6 %collective-permute-start.10 = (bf16[10,64,256]{2,1,0:T(8,128)(2,1)}, bf16[10,64,256]{2,1,0:T(8,128)(2,1)S(1)}, u32[]{:S(2)}, u32[]{:S(2)}) collective-permute-start(bf16[10,64,256]{2,1,0:T(8,128)(2,1)} %get-tuple-element.81), channel_id=1, source_target_pairs={{0,5},{1,4},{2,7},{3,6},{4,1},{5,0},{6,3},{7,2},{8,13},{9,12},{10,... | collective-permute-start | bytes 983048 | tf_op jit(solution)/shard_map/ppermute | solution.py:53
  35.8 18.4 %collective-permute-start.7 = (bf16[2,9,64,128]{3,2,1,0:T(8,128)(2,1)S(1)}, bf16[2,9,64,128]{3,2,1,0:T(8,128)(2,1)S(1)}, u32[]{:S(2)}, u32[]{:S(2)}) collective-permute-start(bf16[2,9,64,128]{3,2,1,0:T(8,128)(2,1)S(1)} %pad_maximum_fusion.8), channel_id=1, source_target_pairs={{0,2},{1,3},{2,0},{3,1},{4,6},{5,7},{6,4},{7,5},{8,10},{9,11},{10,... | collective-permute-start | bytes 884744 | tf_op jit(solution)/shard_map/ppermute | solution.py:53
  38.6 21.9 %collective-permute-start.8 = (bf16[2,9,64,128]{3,2,1,0:T(8,128)(2,1)S(1)}, bf16[2,9,64,128]{3,2,1,0:T(8,128)(2,1)S(1)}, u32[]{:S(2)}, u32[]{:S(2)}) collective-permute-start(bf16[2,9,64,128]{3,2,1,0:T(8,128)(2,1)S(1)} %pad_maximum_fusion.8), channel_id=1, source_target_pairs={{0,3},{1,2},{2,1},{3,0},{4,7},{5,6},{6,5},{7,4},{8,11},{9,10},{10,... | collective-permute-start | bytes 884744 | tf_op jit(solution)/shard_map/ppermute | solution.py:53
  64.2 28.6 %collective-permute-start.11 = (bf16[8,9,64,128]{3,2,1,0:T(8,128)(2,1)S(1)}, bf16[8,9,64,128]{3,2,1,0:T(8,128)(2,1)S(1)}, u32[]{:S(2)}, u32[]{:S(2)}) collective-permute-start(bf16[8,9,64,128]{3,2,1,0:T(8,128)(2,1)S(1)} %constant_dynamic-update-slice_fusion), channel_id=1, source_target_pairs={{0,16},{8,24},{16,0},{24,8},{1,17},{9,25},{17,1},{25,9},{2,18},{10... | collective-permute-start | bytes 3538952 | tf_op jit(solution)/shard_map/ppermute | solution.py:53
  64.6 28.5 %collective-permute-start.2 = (bf16[10,64,256]{2,1,0:T(8,128)(2,1)}, bf16[10,64,256]{2,1,0:T(8,128)(2,1)S(1)}, u32[]{:S(2)}, u32[]{:S(2)}) collective-permute-start(bf16[10,64,256]{2,1,0:T(8,128)(2,1)} %get-tuple-element.75), channel_id=1, source_target_pairs={{0,6},{1,7},{2,4},{3,5},{4,2},{5,3},{6,0},{7,1},{8,14},{9,15},{10,... | collective-permute-start | bytes 983048 | tf_op jit(solution)/shard_map/ppermute | solution.py:53
  72.9 20.3 %collective-permute-start.12 = (bf16[10,64,256]{2,1,0:T(8,128)(2,1)}, bf16[10,64,256]{2,1,0:T(8,128)(2,1)S(1)}, u32[]{:S(2)}, u32[]{:S(2)}) collective-permute-start(bf16[10,64,256]{2,1,0:T(8,128)(2,1)} %get-tuple-element.83), channel_id=1, source_target_pairs={{0,7},{1,6},{2,5},{3,4},{4,3},{5,2},{6,1},{7,0},{8,15},{9,14},{10,... | collective-permute-start | bytes 983048 | tf_op jit(solution)/shard_map/ppermute | solution.py:53
  72.9 20.3 %collective-permute-start.13 = (bf16[10,64,256]{2,1,0:T(8,128)(2,1)}, bf16[10,64,256]{2,1,0:T(8,128)(2,1)S(1)}, u32[]{:S(2)}, u32[]{:S(2)}) collective-permute-start(bf16[10,64,256]{2,1,0:T(8,128)(2,1)} %get-tuple-element.84), channel_id=1, source_target_pairs={{0,1},{1,0},{2,3},{3,2},{4,5},{5,4},{6,7},{7,6},{8,9},{9,8},{10,11... | collective-permute-start | bytes 983048 | tf_op jit(solution)/shard_map/ppermute | solution.py:53
  74.3 18.8 %collective-permute-start.14 = (bf16[10,64,256]{2,1,0:T(8,128)(2,1)S(1)}, bf16[10,64,256]{2,1,0:T(8,128)(2,1)S(1)}, u32[]{:S(2)}, u32[]{:S(2)}) collective-permute-start(bf16[10,64,256]{2,1,0:T(8,128)(2,1)S(1)} %copy-done.54), channel_id=1, source_target_pairs={{0,2},{1,3},{2,0},{3,1},{4,6},{5,7},{6,4},{7,5},{8,10},{9,11},{10,... | collective-permute-start | bytes 983048 | tf_op jit(solution)/shard_map/ppermute | solution.py:53
  93.2 20.1 %collective-permute-start.15 = (bf16[16,9,64,128]{3,2,1,0:T(8,128)(2,1)S(1)}, bf16[16,9,64,128]{3,2,1,0:T(8,128)(2,1)}, u32[]{:S(2)}, u32[]{:S(2)}) collective-permute-start(bf16[16,9,64,128]{3,2,1,0:T(8,128)(2,1)S(1)} %pad_maximum_fusion.refs_0_), channel_id=1, source_target_pairs={{0,8},{8,0},{16,24},{24,16},{1,9},{9,1},{17,25},{25,17},{2,10},{10... | collective-permute-start | bytes 7077896 | tf_op jit(solution)/shard_map/ppermute | solution.py:53
  95.0 9.9 %collective-permute-start.3 = (bf16[64,2,7,256]{3,0,2,1:T(8,128)(2,1)S(1)}, bf16[64,2,7,256]{3,0,2,1:T(8,128)(2,1)}, u32[]{:S(2)}, u32[]{:S(2)}) collective-permute-start(bf16[64,2,7,256]{3,0,2,1:T(8,128)(2,1)S(1)} %get-tuple-element.177), channel_id=1, source_target_pairs={{0,8},{8,16},{16,24},{1,9},{9,17},{17,25},{2,10},{10,18},{18,26},{... | collective-permute-start | bytes 1376264 | tf_op jit(solution)/shard_map/ppermute | solution.py:49
  99.7 13.6 %collective-permute-start.16 = (bf16[10,64,256]{2,1,0:T(8,128)(2,1)}, bf16[10,64,256]{2,1,0:T(8,128)(2,1)S(1)}, u32[]{:S(2)}, u32[]{:S(2)}) collective-permute-start(bf16[10,64,256]{2,1,0:T(8,128)(2,1)} %get-tuple-element.87), channel_id=1, source_target_pairs={{0,3},{1,2},{2,1},{3,0},{4,7},{5,6},{6,5},{7,4},{8,11},{9,10},{10,... | collective-permute-start | bytes 983048 | tf_op jit(solution)/shard_map/ppermute | solution.py:53
  130.3 23.4 %collective-permute-start.17 = (bf16[8,64,256]{2,1,0:T(8,128)(2,1)}, bf16[8,64,256]{2,1,0:T(8,128)(2,1)S(1)}, u32[]{:S(2)}, u32[]{:S(2)}) collective-permute-start(bf16[8,64,256]{2,1,0:T(8,128)(2,1)} %get-tuple-element.89), channel_id=1, source_target_pairs={{0,4},{1,5},{2,6},{3,7},{4,0},{5,1},{6,2},{7,3},{8,12},{9,13},{10,... | collective-permute-start | bytes 786440 | tf_op jit(solution)/shard_map/ppermute | solution.py:53
  134.8 18.9 %collective-permute-start.18 = (bf16[8,64,256]{2,1,0:T(8,128)(2,1)}, bf16[8,64,256]{2,1,0:T(8,128)(2,1)S(1)}, u32[]{:S(2)}, u32[]{:S(2)}) collective-permute-start(bf16[8,64,256]{2,1,0:T(8,128)(2,1)} %get-tuple-element.90), channel_id=1, source_target_pairs={{0,1},{1,0},{2,3},{3,2},{4,5},{5,4},{6,7},{7,6},{8,9},{9,8},{10,11... | collective-permute-start | bytes 786440 | tf_op jit(solution)/shard_map/ppermute | solution.py:53
  138.1 26.7 %collective-permute-start.19 = (bf16[8,64,256]{2,1,0:T(8,128)(2,1)}, bf16[8,64,256]{2,1,0:T(8,128)(2,1)S(1)}, u32[]{:S(2)}, u32[]{:S(2)}) collective-permute-start(bf16[8,64,256]{2,1,0:T(8,128)(2,1)} %get-tuple-element.91), channel_id=1, source_target_pairs={{0,5},{1,4},{2,7},{3,6},{4,1},{5,0},{6,3},{7,2},{8,13},{9,12},{10,... | collective-permute-start | bytes 786440 | tf_op jit(solution)/shard_map/ppermute | solution.py:53
  139.2 25.6 %collective-permute-start.20 = (bf16[8,64,256]{2,1,0:T(8,128)(2,1)}, bf16[8,64,256]{2,1,0:T(8,128)(2,1)}, u32[]{:S(2)}, u32[]{:S(2)}) collective-permute-start(bf16[8,64,256]{2,1,0:T(8,128)(2,1)} %get-tuple-element.92), channel_id=1, source_target_pairs={{0,2},{1,3},{2,0},{3,1},{4,6},{5,7},{6,4},{7,5},{8,10},{9,11},{10,... | collective-permute-start | bytes 786440 | tf_op jit(solution)/shard_map/ppermute | solution.py:53
  140.8 23.9 %collective-permute-start.21 = (bf16[8,64,256]{2,1,0:T(8,128)(2,1)}, bf16[8,64,256]{2,1,0:T(8,128)(2,1)}, u32[]{:S(2)}, u32[]{:S(2)}) collective-permute-start(bf16[8,64,256]{2,1,0:T(8,128)(2,1)} %get-tuple-element.93), channel_id=1, source_target_pairs={{0,6},{1,7},{2,4},{3,5},{4,2},{5,3},{6,0},{7,1},{8,14},{9,15},{10,... | collective-permute-start | bytes 786440 | tf_op jit(solution)/shard_map/ppermute | solution.py:53
  153.7 21.6 %collective-permute-start.22 = (bf16[8,64,256]{2,1,0:T(8,128)(2,1)}, bf16[8,64,256]{2,1,0:T(8,128)(2,1)}, u32[]{:S(2)}, u32[]{:S(2)}) collective-permute-start(bf16[8,64,256]{2,1,0:T(8,128)(2,1)} %get-tuple-element.94), channel_id=1, source_target_pairs={{0,3},{1,2},{2,1},{3,0},{4,7},{5,6},{6,5},{7,4},{8,11},{9,10},{10,... | collective-permute-start | bytes 786440 | tf_op jit(solution)/shard_map/ppermute | solution.py:53
  153.7 21.6 %collective-permute-start.23 = (bf16[8,64,256]{2,1,0:T(8,128)(2,1)}, bf16[8,64,256]{2,1,0:T(8,128)(2,1)}, u32[]{:S(2)}, u32[]{:S(2)}) collective-permute-start(bf16[8,64,256]{2,1,0:T(8,128)(2,1)} %get-tuple-element.95), channel_id=1, source_target_pairs={{0,7},{1,6},{2,5},{3,4},{4,3},{5,2},{6,1},{7,0},{8,15},{9,14},{10,... | collective-permute-start | bytes 786440 | tf_op jit(solution)/shard_map/ppermute | solution.py:53
  178.5 188.7 %reduce-scatter.2.cloned.1.call-start = ((), (), s32[]{:S(2)}) async-start(), calls=%async_computation.1 | async-start | bytes 5898240 | tf_op jit(solution)/shard_map/reduce_scatter | solution.py:841
  210.2 37.8 %collective-permute-start.29 = (bf16[10,32,256]{2,1,0:T(8,128)(2,1)}, bf16[10,32,256]{2,1,0:T(8,128)(2,1)S(1)}, u32[]{:S(2)}, u32[]{:S(2)}) collective-permute-start(bf16[10,32,256]{2,1,0:T(8,128)(2,1)} %get-tuple-element.105), channel_id=1, source_target_pairs={{0,4},{1,5},{2,6},{3,7},{4,0},{5,1},{6,2},{7,3},{8,12},{9,13},{10,... | collective-permute-start | bytes 491528 | tf_op jit(solution)/shard_map/ppermute | solution.py:53
  217.6 31.5 %collective-permute-start.30 = (bf16[10,32,256]{2,1,0:T(8,128)(2,1)}, bf16[10,32,256]{2,1,0:T(8,128)(2,1)S(1)}, u32[]{:S(2)}, u32[]{:S(2)}) collective-permute-start(bf16[10,32,256]{2,1,0:T(8,128)(2,1)} %get-tuple-element.106), channel_id=1, source_target_pairs={{0,5},{1,4},{2,7},{3,6},{4,1},{5,0},{6,3},{7,2},{8,13},{9,12},{10,... | collective-permute-start | bytes 491528 | tf_op jit(solution)/shard_map/ppermute | solution.py:53
  217.7 33.4 %collective-permute-start.31 = (bf16[10,32,256]{2,1,0:T(8,128)(2,1)}, bf16[10,32,256]{2,1,0:T(8,128)(2,1)S(1)}, u32[]{:S(2)}, u32[]{:S(2)}) collective-permute-start(bf16[10,32,256]{2,1,0:T(8,128)(2,1)} %get-tuple-element.107), channel_id=1, source_target_pairs={{0,6},{1,7},{2,4},{3,5},{4,2},{5,3},{6,0},{7,1},{8,14},{9,15},{10,... | collective-permute-start | bytes 491528 | tf_op jit(solution)/shard_map/ppermute | solution.py:53
  219.8 31.3 %collective-permute-start.32 = (bf16[10,32,256]{2,1,0:T(8,128)(2,1)}, bf16[10,32,256]{2,1,0:T(8,128)(2,1)S(1)}, u32[]{:S(2)}, u32[]{:S(2)}) collective-permute-start(bf16[10,32,256]{2,1,0:T(8,128)(2,1)} %get-tuple-element.108), channel_id=1, source_target_pairs={{0,7},{1,6},{2,5},{3,4},{4,3},{5,2},{6,1},{7,0},{8,15},{9,14},{10,... | collective-permute-start | bytes 491528 | tf_op jit(solution)/shard_map/ppermute | solution.py:53
  223.2 32.4 %collective-permute-start.26 = (bf16[10,32,256]{2,1,0:T(8,128)(2,1)}, bf16[10,32,256]{2,1,0:T(8,128)(2,1)S(1)}, u32[]{:S(2)}, u32[]{:S(2)}) collective-permute-start(bf16[10,32,256]{2,1,0:T(8,128)(2,1)} %get-tuple-element.102), channel_id=1, source_target_pairs={{0,1},{1,0},{2,3},{3,2},{4,5},{5,4},{6,7},{7,6},{8,9},{9,8},{10,11... | collective-permute-start | bytes 491528 | tf_op jit(solution)/shard_map/ppermute | solution.py:53
  249.2 9.0 %collective-permute-start.28 = (bf16[10,32,256]{2,1,0:T(8,128)(2,1)S(1)}, bf16[10,32,256]{2,1,0:T(8,128)(2,1)S(1)}, u32[]{:S(2)}, u32[]{:S(2)}) collective-permute-start(bf16[10,32,256]{2,1,0:T(8,128)(2,1)S(1)} %copy-done.59), channel_id=1, source_target_pairs={{0,3},{1,2},{2,1},{3,0},{4,7},{5,6},{6,5},{7,4},{8,11},{9,10},{10,... | collective-permute-start | bytes 491528 | tf_op jit(solution)/shard_map/ppermute | solution.py:53
  251.7 10.8 %collective-permute-start.34 = (bf16[10,32,256]{2,1,0:T(8,128)(2,1)}, bf16[10,32,256]{2,1,0:T(8,128)(2,1)S(1)}, u32[]{:S(2)}, u32[]{:S(2)}) collective-permute-start(bf16[10,32,256]{2,1,0:T(8,128)(2,1)} %get-tuple-element.114), channel_id=1, source_target_pairs={{0,2},{1,3},{2,0},{3,1},{4,6},{5,7},{6,4},{7,5},{8,10},{9,11},{10,... | collective-permute-start | bytes 491528 | tf_op jit(solution)/shard_map/ppermute | solution.py:53
  255.5 24.4 %collective-permute-start.35 = (bf16[10,32,256]{2,1,0:T(8,128)(2,1)}, bf16[10,32,256]{2,1,0:T(8,128)(2,1)S(1)}, u32[]{:S(2)}, u32[]{:S(2)}) collective-permute-start(bf16[10,32,256]{2,1,0:T(8,128)(2,1)} %get-tuple-element.116), channel_id=1, source_target_pairs={{0,3},{1,2},{2,1},{3,0},{4,7},{5,6},{6,5},{7,4},{8,11},{9,10},{10,... | collective-permute-start | bytes 491528 | tf_op jit(solution)/shard_map/ppermute | solution.py:53
  255.6 24.4 %collective-permute-start.36 = (bf16[10,32,256]{2,1,0:T(8,128)(2,1)}, bf16[10,32,256]{2,1,0:T(8,128)(2,1)S(1)}, u32[]{:S(2)}, u32[]{:S(2)}) collective-permute-start(bf16[10,32,256]{2,1,0:T(8,128)(2,1)} %get-tuple-element.118), channel_id=1, source_target_pairs={{0,4},{1,5},{2,6},{3,7},{4,0},{5,1},{6,2},{7,3},{8,12},{9,13},{10,... | collective-permute-start | bytes 491528 | tf_op jit(solution)/shard_map/ppermute | solution.py:53
  258.2 21.9 %collective-permute-start.37 = (bf16[10,32,256]{2,1,0:T(8,128)(2,1)}, bf16[10,32,256]{2,1,0:T(8,128)(2,1)S(1)}, u32[]{:S(2)}, u32[]{:S(2)}) collective-permute-start(bf16[10,32,256]{2,1,0:T(8,128)(2,1)} %get-tuple-element.120), channel_id=1, source_target_pairs={{0,5},{1,4},{2,7},{3,6},{4,1},{5,0},{6,3},{7,2},{8,13},{9,12},{10,... | collective-permute-start | bytes 491528 | tf_op jit(solution)/shard_map/ppermute | solution.py:53
  259.4 20.6 %collective-permute-start.38 = (bf16[10,32,256]{2,1,0:T(8,128)(2,1)}, bf16[10,32,256]{2,1,0:T(8,128)(2,1)S(1)}, u32[]{:S(2)}, u32[]{:S(2)}) collective-permute-start(bf16[10,32,256]{2,1,0:T(8,128)(2,1)} %get-tuple-element.122), channel_id=1, source_target_pairs={{0,6},{1,7},{2,4},{3,5},{4,2},{5,3},{6,0},{7,1},{8,14},{9,15},{10,... | collective-permute-start | bytes 491528 | tf_op jit(solution)/shard_map/ppermute | solution.py:53
  262.5 18.0 %collective-permute-start.39 = (bf16[10,32,256]{2,1,0:T(8,128)(2,1)}, bf16[10,32,256]{2,1,0:T(8,128)(2,1)S(1)}, u32[]{:S(2)}, u32[]{:S(2)}) collective-permute-start(bf16[10,32,256]{2,1,0:T(8,128)(2,1)} %get-tuple-element.124), channel_id=1, source_target_pairs={{0,7},{1,6},{2,5},{3,4},{4,3},{5,2},{6,1},{7,0},{8,15},{9,14},{10,... | collective-permute-start | bytes 491528 | tf_op jit(solution)/shard_map/ppermute | solution.py:53
  310.7 42.3 %collective-permute-start.40 = (bf16[8,64,256]{2,1,0:T(8,128)(2,1)}, bf16[8,64,256]{2,1,0:T(8,128)(2,1)S(1)}, u32[]{:S(2)}, u32[]{:S(2)}) collective-permute-start(bf16[8,64,256]{2,1,0:T(8,128)(2,1)} %get-tuple-element.127), channel_id=1, source_target_pairs={{0,4},{1,5},{2,6},{3,7},{4,0},{5,1},{6,2},{7,3},{8,12},{9,13},{10,... | collective-permute-start | bytes 786440 | tf_op jit(solution)/shard_map/ppermute | solution.py:53
  316.9 36.9 %collective-permute-start.41 = (bf16[8,64,256]{2,1,0:T(8,128)(2,1)S(1)}, bf16[8,64,256]{2,1,0:T(8,128)(2,1)S(1)}, u32[]{:S(2)}, u32[]{:S(2)}) collective-permute-start(bf16[8,64,256]{2,1,0:T(8,128)(2,1)S(1)} %copy-done.58), channel_id=1, source_target_pairs={{0,5},{1,4},{2,7},{3,6},{4,1},{5,0},{6,3},{7,2},{8,13},{9,12},{10,... | collective-permute-start | bytes 786440 | tf_op jit(solution)/shard_map/ppermute | solution.py:53
  319.4 41.4 %collective-permute-start.42 = (bf16[8,64,256]{2,1,0:T(8,128)(2,1)}, bf16[8,64,256]{2,1,0:T(8,128)(2,1)S(1)}, u32[]{:S(2)}, u32[]{:S(2)}) collective-permute-start(bf16[8,64,256]{2,1,0:T(8,128)(2,1)} %get-tuple-element.129), channel_id=1, source_target_pairs={{0,6},{1,7},{2,4},{3,5},{4,2},{5,3},{6,0},{7,1},{8,14},{9,15},{10,... | collective-permute-start | bytes 786440 | tf_op jit(solution)/shard_map/ppermute | solution.py:53
  320.3 40.5 %collective-permute-start.43 = (bf16[8,64,256]{2,1,0:T(8,128)(2,1)}, bf16[8,64,256]{2,1,0:T(8,128)(2,1)S(1)}, u32[]{:S(2)}, u32[]{:S(2)}) collective-permute-start(bf16[8,64,256]{2,1,0:T(8,128)(2,1)} %get-tuple-element.130), channel_id=1, source_target_pairs={{0,7},{1,6},{2,5},{3,4},{4,3},{5,2},{6,1},{7,0},{8,15},{9,14},{10,... | collective-permute-start | bytes 786440 | tf_op jit(solution)/shard_map/ppermute | solution.py:53
  323.2 37.7 %collective-permute-start.44 = (bf16[8,64,256]{2,1,0:T(8,128)(2,1)S(1)}, bf16[8,64,256]{2,1,0:T(8,128)(2,1)S(1)}, u32[]{:S(2)}, u32[]{:S(2)}) collective-permute-start(bf16[8,64,256]{2,1,0:T(8,128)(2,1)S(1)} %copy-done.57), channel_id=1, source_target_pairs={{0,1},{1,0},{2,3},{3,2},{4,5},{5,4},{6,7},{7,6},{8,9},{9,8},{10,11... | collective-permute-start | bytes 786440 | tf_op jit(solution)/shard_map/ppermute | solution.py:53
  353.0 9.3 %collective-permute-start.45 = (bf16[8,64,256]{2,1,0:T(8,128)(2,1)S(1)}, bf16[8,64,256]{2,1,0:T(8,128)(2,1)S(1)}, u32[]{:S(2)}, u32[]{:S(2)}) collective-permute-start(bf16[8,64,256]{2,1,0:T(8,128)(2,1)S(1)} %copy-done.56), channel_id=1, source_target_pairs={{0,2},{1,3},{2,0},{3,1},{4,6},{5,7},{6,4},{7,5},{8,10},{9,11},{10,... | collective-permute-start | bytes 786440 | tf_op jit(solution)/shard_map/ppermute | solution.py:53
  353.8 13.4 %collective-permute-start.46 = (bf16[8,64,256]{2,1,0:T(8,128)(2,1)S(1)}, bf16[8,64,256]{2,1,0:T(8,128)(2,1)S(1)}, u32[]{:S(2)}, u32[]{:S(2)}) collective-permute-start(bf16[8,64,256]{2,1,0:T(8,128)(2,1)S(1)} %copy-done.55), channel_id=1, source_target_pairs={{0,3},{1,2},{2,1},{3,0},{4,7},{5,6},{6,5},{7,4},{8,11},{9,10},{10,... | collective-permute-start | bytes 786440 | tf_op jit(solution)/shard_map/ppermute | solution.py:53
  368.9 14.7 %collective-permute-start.53 = (bf16[608,128]{1,0:T(8,128)(2,1)S(1)}, bf16[608,128]{1,0:T(8,128)(2,1)S(1)}, u32[]{:S(2)}, u32[]{:S(2)}) collective-permute-start(bf16[608,128]{1,0:T(8,128)(2,1)S(1)} %get-tuple-element.193), channel_id=1, source_target_pairs={{0,7},{1,6},{2,5},{3,4},{4,3},{5,2},{6,1},{7,0},{8,15},{9,14},{10,... | collective-permute-start | bytes 466952 | tf_op jit(solution)/shard_map/ppermute | solution.py:53
  376.7 9.0 %collective-permute-start.51 = (bf16[608,128]{1,0:T(8,128)(2,1)S(1)}, bf16[608,128]{1,0:T(8,128)(2,1)S(1)}, u32[]{:S(2)}, u32[]{:S(2)}) collective-permute-start(bf16[608,128]{1,0:T(8,128)(2,1)S(1)} %get-tuple-element.191), channel_id=1, source_target_pairs={{0,6},{1,7},{2,4},{3,5},{4,2},{5,3},{6,0},{7,1},{8,14},{9,15},{10,... | collective-permute-start | bytes 466952 | tf_op jit(solution)/shard_map/ppermute | solution.py:53
  379.8 17.5 %collective-permute-start.49 = (bf16[608,128]{1,0:T(8,128)(2,1)S(1)}, bf16[608,128]{1,0:T(8,128)(2,1)S(1)}, u32[]{:S(2)}, u32[]{:S(2)}) collective-permute-start(bf16[608,128]{1,0:T(8,128)(2,1)S(1)} %get-tuple-element.189), channel_id=1, source_target_pairs={{0,5},{1,4},{2,7},{3,6},{4,1},{5,0},{6,3},{7,2},{8,13},{9,12},{10,... | collective-permute-start | bytes 466952 | tf_op jit(solution)/shard_map/ppermute | solution.py:53
  381.2 18.6 %collective-permute-start.47 = (bf16[608,128]{1,0:T(8,128)(2,1)S(1)}, bf16[608,128]{1,0:T(8,128)(2,1)S(1)}, u32[]{:S(2)}, u32[]{:S(2)}) collective-permute-start(bf16[608,128]{1,0:T(8,128)(2,1)S(1)} %get-tuple-element.194), channel_id=1, source_target_pairs={{0,4},{1,5},{2,6},{3,7},{4,0},{5,1},{6,2},{7,3},{8,12},{9,13},{10,... | collective-permute-start | bytes 466952 | tf_op jit(solution)/shard_map/ppermute | solution.py:53
  382.1 17.8 %collective-permute-start.52 = (bf16[608,128]{1,0:T(8,128)(2,1)S(1)}, bf16[608,128]{1,0:T(8,128)(2,1)S(1)}, u32[]{:S(2)}, u32[]{:S(2)}) collective-permute-start(bf16[608,128]{1,0:T(8,128)(2,1)S(1)} %get-tuple-element.192), channel_id=1, source_target_pairs={{0,3},{1,2},{2,1},{3,0},{4,7},{5,6},{6,5},{7,4},{8,11},{9,10},{10,... | collective-permute-start | bytes 466952 | tf_op jit(solution)/shard_map/ppermute | solution.py:53
  383.6 16.3 %collective-permute-start.50 = (bf16[608,128]{1,0:T(8,128)(2,1)S(1)}, bf16[608,128]{1,0:T(8,128)(2,1)S(1)}, u32[]{:S(2)}, u32[]{:S(2)}) collective-permute-start(bf16[608,128]{1,0:T(8,128)(2,1)S(1)} %get-tuple-element.190), channel_id=1, source_target_pairs={{0,2},{1,3},{2,0},{3,1},{4,6},{5,7},{6,4},{7,5},{8,10},{9,11},{10,... | collective-permute-start | bytes 466952 | tf_op jit(solution)/shard_map/ppermute | solution.py:53
  385.7 14.2 %collective-permute-start.48 = (bf16[608,128]{1,0:T(8,128)(2,1)S(1)}, bf16[608,128]{1,0:T(8,128)(2,1)S(1)}, u32[]{:S(2)}, u32[]{:S(2)}) collective-permute-start(bf16[608,128]{1,0:T(8,128)(2,1)S(1)} %get-tuple-element.188), channel_id=1, source_target_pairs={{0,1},{1,0},{2,3},{3,2},{4,5},{5,4},{6,7},{7,6},{8,9},{9,8},{10,11... | collective-permute-start | bytes 466952 | tf_op jit(solution)/shard_map/ppermute | solution.py:53
  400.3 8.7 %collective-permute-start.55 = (bf16[608,128]{1,0:T(8,128)(2,1)S(1)}, bf16[608,128]{1,0:T(8,128)(2,1)S(1)}, u32[]{:S(2)}, u32[]{:S(2)}) collective-permute-start(bf16[608,128]{1,0:T(8,128)(2,1)S(1)} %fusion.18.refs_0_), channel_id=1, source_target_pairs={{0,16},{8,24},{16,0},{24,8},{1,17},{9,25},{17,1},{25,9},{2,18},{10... | collective-permute-start | bytes 466952 | tf_op jit(solution)/shard_map/ppermute | solution.py:53
  (73 other events, 779.7 us)
Sparse Core Ops, SparseCore 0:
  178.6 70.0 all-gather.1
Sparse Core Ops, SparseCore 1:
  309.6 54.9 reduce-scatter.1
